TPU v7x, 32 devices: a whole 2x2x4 slice. The times are simulated.
32 devices in a mesh: batch: 16 (over z, y, x), pair: 2 (over core).
Axes of the slice: x: 2, y: 2, z: 4, core: 2. Of those that a mesh axis runs over, the one named last changes fastest.
Arguments:
- tokens: bfloat16 [64, 2, 160, 768], P('batch', 'pair'), may hold values from -6 to 6
- segment_ids: int32 [64, 2, 160], P('batch'), may hold values from -1 to 2, as said below
- query_weight: bfloat16 [768, 768], P(('batch', 'pair')), may hold values from -0.21875 to 0.21875
- query_bias: bfloat16 [768], P(('batch', 'pair')), may hold values from -3 to 3
- key_weight: bfloat16 [768, 768], P(('batch', 'pair')), may hold values from -0.21875 to 0.21875
- value_weight: bfloat16 [768, 768], P(('batch', 'pair')), may hold values from -0.21875 to 0.21875
- value_bias: bfloat16 [768], P(('batch', 'pair')), may hold values from -3 to 3
- out_weight: bfloat16 [768, 768], P(('batch', 'pair')), may hold values from -1.25 to 1.25
- out_bias: bfloat16 [768], P(('batch', 'pair')), may hold values from -3 to 3
- first_gain: bfloat16 [768], P(('batch', 'pair')), may hold values from 0.5 to 1.5
- first_shift: bfloat16 [768], P(('batch', 'pair')), may hold values from -2 to 2
- up_weight: bfloat16 [768, 3072], P(('batch', 'pair')), may hold values from -0.21875 to 0.21875
- up_bias: bfloat16 [3072], P(('batch', 'pair')), may hold values from -3 to 3
- down_weight: bfloat16 [3072, 768], P(('batch', 'pair')), may hold values from -0.109375 to 0.109375
- down_bias: bfloat16 [768], P(('batch', 'pair')), may hold values from -2 to 2
- second_gain: bfloat16 [768], P(('batch', 'pair')), may hold values from 0.5 to 1.5
- second_shift: bfloat16 [768], P(('batch', 'pair')), may hold values from -2 to 2
- cotangent: bfloat16 [64, 2, 160, 768], P('batch', 'pair'), may hold values from -6 to 6
Outputs:
- layer_output: bfloat16 [64, 2, 160, 768], P('batch', 'pair')
- tokens_gradient: bfloat16 [64, 2, 160, 768], P('batch', 'pair')
- query_weight_gradient: float32 [768, 768], P(('batch', 'pair'))
- query_bias_gradient: float32 [768], P(('batch', 'pair'))
- key_weight_gradient: float32 [768, 768], P(('batch', 'pair'))
- value_weight_gradient: float32 [768, 768], P(('batch', 'pair'))
- value_bias_gradient: float32 [768], P(('batch', 'pair'))
- out_weight_gradient: float32 [768, 768], P(('batch', 'pair'))
- out_bias_gradient: float32 [768], P(('batch', 'pair'))
- first_gain_gradient: float32 [768], P(('batch', 'pair'))
- first_shift_gradient: float32 [768], P(('batch', 'pair'))
- up_weight_gradient: float32 [768, 3072], P(('batch', 'pair'))
- up_bias_gradient: float32 [3072], P(('batch', 'pair'))
- down_weight_gradient: float32 [3072, 768], P(('batch', 'pair'))
- down_bias_gradient: float32 [768], P(('batch', 'pair'))
- second_gain_gradient: float32 [768], P(('batch', 'pair'))
- second_shift_gradient: float32 [768], P(('batch', 'pair'))
Inputs may be any that keep to these rules, and one draw needn't show every extreme that they name: `segment_ids`: within each half of a sequence the ids never fall, pairs are numbered from 0 and each pair holds at least one word slot and one region slot; a sequence holds 2 or 3 pairs; -1 appears only after the last pair of a half, and word slots 96 and later are always -1.
All inputs are finite; a program needn't handle non-finite values.
Results may differ from a plain program's by a relative error of at most 0.014.
Values may be sent and summed in bfloat16 or wider, within the bound.
A program may use at most 192 MiB of HBM per device.

v0:
```python
import jax
import jax.numpy as jnp
from jax import lax
from jax.sharding import PartitionSpec as P

HEAD_DIM = 64


EPSILON = 1e-05
NEG_FILL = -1e30


def swapped(value, axis, stride):
    return lax.ppermute(value, axis, [(i, i ^ 1 << stride) for i in range(lax.axis_size(axis))])


def layer_norm(values, gain, shift):
    average = jnp.mean(values, -1, keepdims=True)
    centred = values - average
    variance = jnp.mean(centred * centred, -1, keepdims=True)
    return centred * lax.rsqrt(variance + EPSILON) * gain + shift


def matmul(left, right):
    return jnp.dot(left, right, preferred_element_type=jnp.float32)


def product_back(left, right):
    return lax.dot_general(
        left, right, (((left.ndim - 1,), (1,)), ((), ())), preferred_element_type=jnp.float32
    )


def outer_sum(left, right):
    flat_left = left.reshape(-1, left.shape[-1])
    flat_right = right.reshape(-1, right.shape[-1])
    return lax.dot_general(
        flat_left, flat_right, (((0,), (0,)), ((), ())), preferred_element_type=jnp.float32
    )


def row_total(values):
    return jnp.sum(values.astype(jnp.float32), (0, 1))


def scores_of(query_heads, key_rows, allowed, factor):
    raw = jnp.einsum("sqhd,skhd->shqk", query_heads, key_rows, preferred_element_type=jnp.float32)
    return jnp.where(allowed, raw * factor, NEG_FILL)


def local(
    tokens,
    segment_ids,
    query_weight,
    query_bias,
    key_weight,
    value_weight,
    value_bias,
    out_weight,
    out_bias,
    first_gain,
    first_shift,
    up_weight,
    up_bias,
    down_weight,
    down_bias,
    second_gain,
    second_shift,
    cotangent,
):
    seqs = tokens.shape[0]
    slots = tokens.shape[2]
    width = tokens.shape[3]
    heads = width // HEAD_DIM
    factor = HEAD_DIM ** (-0.5)
    token_rows = tokens.reshape(seqs, slots, width)
    attention_shards = (
        query_weight,
        query_bias,
        key_weight,
        value_weight,
        value_bias,
        out_weight,
        out_bias,
        first_gain,
        first_shift,
    )
    feedforward_shards = (up_weight, up_bias, down_weight, down_bias, second_gain, second_shift)
    attention_full = (
        lax.all_gather(attention_shards[0], ("batch", "pair"), axis=0, tiled=True),
        lax.all_gather(attention_shards[1], ("batch", "pair"), axis=0, tiled=True),
        lax.all_gather(attention_shards[2], ("batch", "pair"), axis=0, tiled=True),
        lax.all_gather(attention_shards[3], ("batch", "pair"), axis=0, tiled=True),
        lax.all_gather(attention_shards[4], ("batch", "pair"), axis=0, tiled=True),
        lax.all_gather(attention_shards[5], ("batch", "pair"), axis=0, tiled=True),
        lax.all_gather(attention_shards[6], ("batch", "pair"), axis=0, tiled=True),
        lax.all_gather(attention_shards[7], ("batch", "pair"), axis=0, tiled=True),
        lax.all_gather(attention_shards[8], ("batch", "pair"), axis=0, tiled=True),
    )
    feedforward_full = (
        lax.all_gather(feedforward_shards[0], ("batch", "pair"), axis=0, tiled=True),
        lax.all_gather(feedforward_shards[1], ("batch", "pair"), axis=0, tiled=True),
        lax.all_gather(feedforward_shards[2], ("batch", "pair"), axis=0, tiled=True),
        lax.all_gather(feedforward_shards[3], ("batch", "pair"), axis=0, tiled=True),
        lax.all_gather(feedforward_shards[4], ("batch", "pair"), axis=0, tiled=True),
        lax.all_gather(feedforward_shards[5], ("batch", "pair"), axis=0, tiled=True),
    )
    (
        query_mat,
        query_vec,
        key_mat,
        value_mat,
        value_vec,
        out_mat,
        out_vec,
        gain_first,
        shift_first,
    ) = attention_full
    up_mat, up_vec, down_mat, down_vec, gain_second, shift_second = feedforward_full
    pair_index = lax.axis_index("pair")
    own_ids = lax.dynamic_index_in_dim(segment_ids, pair_index, 1, keepdims=False)
    other_ids = lax.dynamic_index_in_dim(segment_ids, 1 - pair_index, 1, keepdims=False)
    key_ids = jnp.concatenate([own_ids, other_ids], 1)
    allowed = (own_ids[:, :, None] == key_ids[:, None, :])[:, None]
    queries = (matmul(token_rows, query_mat) + query_vec).astype(jnp.bfloat16)
    keys_own = matmul(token_rows, key_mat).astype(jnp.bfloat16)
    values_own = (matmul(token_rows, value_mat) + value_vec).astype(jnp.bfloat16)
    keys_other, values_other = swapped((keys_own, values_own), "pair", 0)
    head_rows = (seqs, 2 * slots, heads, HEAD_DIM)
    key_rows = jnp.concatenate([keys_own, keys_other], 1).reshape(head_rows)
    value_rows = jnp.concatenate([values_own, values_other], 1).reshape(head_rows)
    query_heads = queries.reshape(seqs, slots, heads, HEAD_DIM)
    scores = scores_of(query_heads, key_rows, allowed, factor)
    row_max = jnp.max(scores, -1, keepdims=True)
    log_total = row_max + jnp.log(jnp.sum(jnp.exp(scores - row_max), -1, keepdims=True))
    probs_low = jnp.exp(scores - log_total).astype(jnp.bfloat16)
    mixed = jnp.einsum("shqk,skhd->sqhd", probs_low, value_rows, preferred_element_type=jnp.float32)
    mixed = mixed.reshape(seqs, slots, width).astype(jnp.bfloat16)
    first_resid = token_rows.astype(jnp.float32) + matmul(mixed, out_mat) + out_vec
    normed, first_pull = jax.vjp(
        layer_norm, first_resid, gain_first.astype(jnp.float32), shift_first.astype(jnp.float32)
    )
    normed_low = normed.astype(jnp.bfloat16)
    pre_hidden = matmul(normed_low, up_mat) + up_vec
    hidden, gelu_pull = jax.vjp(jax.nn.gelu, pre_hidden)
    hidden_low = hidden.astype(jnp.bfloat16)
    second_resid = normed + matmul(hidden_low, down_mat) + down_vec
    final, second_pull = jax.vjp(
        layer_norm, second_resid, gain_second.astype(jnp.float32), shift_second.astype(jnp.float32)
    )
    layer_output = final.astype(jnp.bfloat16).reshape(tokens.shape)
    out_grad = cotangent.reshape(seqs, slots, width).astype(jnp.float32)
    second_grad, gain_second_grad, shift_second_grad = second_pull(out_grad)
    down_in = second_grad.astype(jnp.bfloat16)
    down_weight_grad = outer_sum(hidden_low, down_in)
    down_bias_grad = row_total(down_in)
    hidden_grad = product_back(down_in, down_mat)
    (pre_grad,) = gelu_pull(hidden_grad)
    pre_low = pre_grad.astype(jnp.bfloat16)
    up_weight_grad = outer_sum(normed_low, pre_low)
    up_bias_grad = row_total(pre_low)
    normed_grad = product_back(pre_low, up_mat) + second_grad
    first_grad, gain_first_grad, shift_first_grad = first_pull(normed_grad)
    feedforward_terms = (
        up_weight_grad,
        up_bias_grad,
        down_weight_grad,
        down_bias_grad,
        gain_second_grad,
        shift_second_grad,
    )
    feedforward_parts = (
        lax.psum_scatter(feedforward_terms[0], ("batch", "pair"), scatter_dimension=0, tiled=True),
        lax.psum_scatter(feedforward_terms[1], ("batch", "pair"), scatter_dimension=0, tiled=True),
        lax.psum_scatter(feedforward_terms[2], ("batch", "pair"), scatter_dimension=0, tiled=True),
        lax.psum_scatter(feedforward_terms[3], ("batch", "pair"), scatter_dimension=0, tiled=True),
        lax.psum_scatter(feedforward_terms[4], ("batch", "pair"), scatter_dimension=0, tiled=True),
        lax.psum_scatter(feedforward_terms[5], ("batch", "pair"), scatter_dimension=0, tiled=True),
    )
    branch_low = first_grad.astype(jnp.bfloat16)
    out_weight_grad = outer_sum(mixed, branch_low)
    out_bias_grad = row_total(branch_low)
    mixed_grad = (
        product_back(branch_low, out_mat).astype(jnp.bfloat16).reshape(seqs, slots, heads, HEAD_DIM)
    )
    scores = scores_of(query_heads, key_rows, allowed, factor)
    probs = jnp.exp(scores - log_total)
    probs_low = probs.astype(jnp.bfloat16)
    probs_grad = jnp.einsum(
        "sqhd,skhd->shqk", mixed_grad, value_rows, preferred_element_type=jnp.float32
    )
    delta = jnp.sum(probs * probs_grad, -1, keepdims=True)
    score_grad = (probs * (probs_grad - delta)).astype(jnp.bfloat16)
    query_grad = (
        jnp.einsum("shqk,skhd->sqhd", score_grad, key_rows, preferred_element_type=jnp.float32)
        * factor
    )
    query_grad = query_grad.reshape(seqs, slots, width).astype(jnp.bfloat16)
    key_grad_all = jnp.einsum(
        "shqk,sqhd->skhd", score_grad, query_heads, preferred_element_type=jnp.float32
    )
    key_grad_all = (key_grad_all * factor).reshape(seqs, 2 * slots, width)
    value_grad_all = jnp.einsum(
        "shqk,sqhd->skhd", probs_low, mixed_grad, preferred_element_type=jnp.float32
    )
    value_grad_all = value_grad_all.reshape(seqs, 2 * slots, width)
    keys_back, values_back = (
        swapped(key_grad_all[:, slots:].astype(jnp.bfloat16), "pair", 0).astype(jnp.float32),
        swapped(value_grad_all[:, slots:].astype(jnp.bfloat16), "pair", 0).astype(jnp.float32),
    )
    key_grad = (key_grad_all[:, :slots] + keys_back).astype(jnp.bfloat16)
    value_grad = (value_grad_all[:, :slots] + values_back).astype(jnp.bfloat16)
    query_weight_grad = outer_sum(token_rows, query_grad)
    query_bias_grad = row_total(query_grad)
    key_weight_grad = outer_sum(token_rows, key_grad)
    value_weight_grad = outer_sum(token_rows, value_grad)
    value_bias_grad = row_total(value_grad)
    tokens_grad = first_grad + product_back(query_grad, query_mat) + product_back(key_grad, key_mat)
    tokens_grad = tokens_grad + product_back(value_grad, value_mat)
    tokens_gradient = tokens_grad.astype(jnp.bfloat16).reshape(tokens.shape)
    attention_terms = (
        query_weight_grad,
        query_bias_grad,
        key_weight_grad,
        value_weight_grad,
        value_bias_grad,
        out_weight_grad,
        out_bias_grad,
        gain_first_grad,
        shift_first_grad,
    )
    attention_parts = (
        lax.psum_scatter(attention_terms[0], ("batch", "pair"), scatter_dimension=0, tiled=True),
        lax.psum_scatter(attention_terms[1], ("batch", "pair"), scatter_dimension=0, tiled=True),
        lax.psum_scatter(attention_terms[2], ("batch", "pair"), scatter_dimension=0, tiled=True),
        lax.psum_scatter(attention_terms[3], ("batch", "pair"), scatter_dimension=0, tiled=True),
        lax.psum_scatter(attention_terms[4], ("batch", "pair"), scatter_dimension=0, tiled=True),
        lax.psum_scatter(attention_terms[5], ("batch", "pair"), scatter_dimension=0, tiled=True),
        lax.psum_scatter(attention_terms[6], ("batch", "pair"), scatter_dimension=0, tiled=True),
        lax.psum_scatter(attention_terms[7], ("batch", "pair"), scatter_dimension=0, tiled=True),
        lax.psum_scatter(attention_terms[8], ("batch", "pair"), scatter_dimension=0, tiled=True),
    )
    return (
        layer_output,
        tokens_gradient,
        attention_parts[0],
        attention_parts[1],
        attention_parts[2],
        attention_parts[3],
        attention_parts[4],
        attention_parts[5],
        attention_parts[6],
        attention_parts[7],
        attention_parts[8],
        feedforward_parts[0],
        feedforward_parts[1],
        feedforward_parts[2],
        feedforward_parts[3],
        feedforward_parts[4],
        feedforward_parts[5],
    )


def solution(mesh):
    in_specs = (
        P("batch", "pair", None, None),
        P("batch", None, None),
        P(("batch", "pair"), None),
        P(("batch", "pair")),
        P(("batch", "pair"), None),
        P(("batch", "pair"), None),
        P(("batch", "pair")),
        P(("batch", "pair"), None),
        P(("batch", "pair")),
        P(("batch", "pair")),
        P(("batch", "pair")),
        P(("batch", "pair"), None),
        P(("batch", "pair")),
        P(("batch", "pair"), None),
        P(("batch", "pair")),
        P(("batch", "pair")),
        P(("batch", "pair")),
        P("batch", "pair", None, None),
    )
    out_specs = (
        P("batch", "pair", None, None),
        P("batch", "pair", None, None),
        P(("batch", "pair"), None),
        P(("batch", "pair")),
        P(("batch", "pair"), None),
        P(("batch", "pair"), None),
        P(("batch", "pair")),
        P(("batch", "pair"), None),
        P(("batch", "pair")),
        P(("batch", "pair")),
        P(("batch", "pair")),
        P(("batch", "pair"), None),
        P(("batch", "pair")),
        P(("batch", "pair"), None),
        P(("batch", "pair")),
        P(("batch", "pair")),
        P(("batch", "pair")),
    )
    return jax.shard_map(local, mesh=mesh, in_specs=in_specs, out_specs=out_specs, check_vma=False)
```

profile of v0, /device:TPU:0, one launch (start us, length us, event | category | flops | bytes accessed | tf_op | source)
XLA Modules:
  0.0 1103.7 jit_solution(2272373561116523066)
XLA Ops:
  18.8 42.4 %all-reduce.19 = (bf16[768]{0:T(1024)(128)(2,1)S(1)}, bf16[768]{0:T(1024)(128)(2,1)S(1)}, bf16[768]{0:T(1024)(128)(2,1)S(1)}, bf16[768]{0:T(1024)(128)(2,1)S(1)}...) all-reduce(bf16[768]{0:T(1024)(128)(2,1)S(1)} %dynamic-update-slice, ...), channel_id=1, replica_groups=mesh['batch'=16,'pair'=2] {'batch','pair'}, use_global_device_ids=true, to_apply=%add | all-reduce | flops 9216 | bytes 36864
  61.2 6.7 all-gather.11.cloned.1.call-done
  67.9 2.5 convolution_convert_fusion.2
  70.8 53.2 %all-gather.7.cloned.1.call-done = bf16[768,768]{1,0:T(8,128)(2,1)} async-done(((bf16[24,768]{1,0:T(8,128)(2,1)}), bf16[768,768]{1,0:T(8,128)(2,1)}) %all-gather.7.cloned.1.call-update) | async-done | bytes 1179664 | tf_op jit(solution)/shard_map/all_gather | solution.py:93
  124.0 3.1 add_convert_fusion.5
  127.8 52.1 %all-gather.9.cloned.1.call-done = bf16[768,768]{1,0:T(8,128)(2,1)} async-done(((bf16[24,768]{1,0:T(8,128)(2,1)}), bf16[768,768]{1,0:T(8,128)(2,1)}) %all-gather.9.cloned.1.call-update) | async-done | bytes 1179664 | tf_op jit(solution)/shard_map/all_gather | solution.py:90
  179.9 2.2 add_convert_fusion.4
  185.0 2.4 copy.76
  189.1 2.4 copy.74
  191.5 5.4 fusion
  196.9 4.5 exponential_reduce_fusion
  201.4 5.8 convolution_convert_fusion
  207.3 28.4 %all-gather.13.cloned.1.call-done = bf16[768,768]{1,0:T(8,128)(2,1)} async-done(((bf16[24,768]{1,0:T(8,128)(2,1)}), bf16[768,768]{1,0:T(8,128)(2,1)}) %all-gather.13.cloned.1.call-update) | async-done | bytes 1179664 | tf_op jit(solution)/shard_map/all_gather | solution.py:95
  235.6 3.2 fusion.59
  239.2 61.8 %all-gather.15.cloned.1.call-done = bf16[768,3072]{1,0:T(8,128)(2,1)} async-done(((bf16[24,3072]{1,0:T(8,128)(2,1)}), bf16[768,3072]{1,0:T(8,128)(2,1)}) %all-gather.15.cloned.1.call-update) | async-done | bytes 4718608 | tf_op jit(solution)/shard_map/all_gather | solution.py:101
  301.0 7.8 fusion.15
  308.8 57.4 %all-gather.17.cloned.1.call-done = bf16[3072,768]{1,0:T(8,128)(2,1)} async-done(((bf16[96,768]{1,0:T(8,128)(2,1)}), bf16[3072,768]{1,0:T(8,128)(2,1)}) %all-gather.17.cloned.1.call-update) | async-done | bytes 4718608 | tf_op jit(solution)/shard_map/all_gather | solution.py:103
  366.2 9.0 fusion.60
  377.7 2.4 convert_reduce_fusion.3
  380.1 8.6 convert_reduce_fusion
  388.7 4.6 multiply_reduce_fusion.1
  396.2 2.6 convolution_bitcast_fusion.2
  402.4 11.9 %multiply_reduce_fusion = (f32[4,12,160]{2,1,0:T(8,128)S(1)}, f32[4,12,160,320]{3,2,1,0:T(8,128)}) fusion(f32[4,12,160,320]{3,2,1,0:T(8,128)} %copy-done, f32[4,12,160]{2,1,0:T(8,128)S(1)} %log_add_fusion, pred[4,160,320]{2,1,0:T(8,128)(4,1)S(1)} %broadcast_compare_fusion, bf16[4,160,12,64]{1,3,2,0:T(8,128)(2,1)S(1)} %bitcast.175, ...), kind=kOutput, calls=%fused_computation.1 | convolution fusion | flops 326853120 | bytes 22876160 | tf_op jit(solution)/shard_map/sqhd,skhd->shqk/dot_general | solution.py:189
  414.4 6.8 multiply_convert_fusion
  421.3 3.3 convert_reduce_fusion.1
  425.8 2.4 copy.85
  428.1 3.1 convert_element_type.165
  431.2 3.7 convolution_bitcast_fusion.5
  434.9 3.1 copy.95
  438.0 7.0 fusion.54
  445.0 2.2 copy-done.4
  449.4 2.1 slice.20
  451.5 2.1 copy.105
  453.7 2.8 convert_reduce_fusion.5
  461.9 3.9 broadcast_multiply_fusion
  465.8 2.1 copy-done.5
  474.4 2.1 add_convert_fusion.2
  480.8 12.2 %convolution_bitcast_fusion = f32[3072,768]{1,0:T(8,128)} fusion(bf16[4,160,768]{2,1,0:T(8,128)(2,1)S(1)} %copy-done.19, f32[4,160,3072]{2,1,0:T(8,128)} %fusion.15, f32[3072]{0:T(1024)S(1)} %copy-done.27), kind=kOutput, calls=%fused_computation.18 | convolution fusion | flops 3039559680 | bytes 18296832 | tf_op jit(solution)/shard_map/dot_general | solution.py:37
  494.5 8.6 convolution_bitcast_fusion.1
  505.2 4.2 fusion.35
  509.4 41.0 %all-reduce.18 = (f32[768]{0:T(1024)S(1)}, f32[768]{0:T(1024)S(1)}, f32[768]{0:T(1024)S(1)}, f32[768]{0:T(1024)S(1)}, f32[768]{0:T(1024)S(1)}, /*index=5*/f32[30...) all-reduce(f32[768]{0:T(1024)} %reduce_sum.216, ...), channel_id=3, replica_groups=mesh['batch'=16,'pair'=2] {'batch','pair'}, use_global_device_ids=true, to_apply=%region_13.14.clone | all-reduce | flops 9216 | bytes 73728
  555.6 2.4 fusion.32
  558.1 3.3 fusion.43
  561.4 43.7 %reduce-scatter.19.cloned.1.call-done = f32[24,768]{1,0:T(8,128)} async-done(((f32[768,768]{1,0:T(8,128)}), f32[24,768]{1,0:T(8,128)}) %reduce-scatter.19.cloned.1.call-update) | async-done | bytes 73744
  605.1 103.9 %reduce-scatter.23.cloned.1.call-done = f32[24,768]{1,0:T(8,128)} async-done(((f32[768,768]{1,0:T(8,128)}), f32[24,768]{1,0:T(8,128)}) %reduce-scatter.23.cloned.1.call-update) | async-done | bytes 73744
  709.0 104.6 %reduce-scatter.21.cloned.1.call-done = f32[24,768]{1,0:T(8,128)} async-done(((f32[768,768]{1,0:T(8,128)}), f32[24,768]{1,0:T(8,128)}) %reduce-scatter.21.cloned.1.call-update) | async-done | bytes 73744
  813.7 141.0 %reduce-scatter.17.cloned.1.call-done = f32[96,768]{1,0:T(8,128)} async-done(((f32[3072,768]{1,0:T(8,128)}), f32[96,768]{1,0:T(8,128)}) %reduce-scatter.17.cloned.1.call-update) | async-done | bytes 294928 | tf_op jit(solution)/shard_map/reduce_scatter | solution.py:175
  954.6 141.8 %reduce-scatter.15.cloned.1.call-done = f32[24,3072]{1,0:T(8,128)} async-done(((f32[768,3072]{1,0:T(8,128)}), f32[24,3072]{1,0:T(8,128)}) %reduce-scatter.15.cloned.1.call-update) | async-done | bytes 294928 | tf_op jit(solution)/shard_map/reduce_scatter | solution.py:173
  (189 shorter events, 54.8 us)
Async XLA Ops:
  7.2 60.7 %all-gather.11.cloned.1.call-start = ((), (), s32[]{:S(2)}) async-start(), calls=%async_computation.8 | async-start | bytes 1216512 | tf_op jit(solution)/shard_map/all_gather | solution.py:92
  7.9 116.1 %all-gather.7.cloned.1.call-start = ((), (), s32[]{:S(2)}) async-start(), calls=%async_computation.6 | async-start | bytes 1216512 | tf_op jit(solution)/shard_map/all_gather | solution.py:93
  8.7 171.2 %all-gather.9.cloned.1.call-start = ((), (), s32[]{:S(2)}) async-start(), calls=%async_computation.7 | async-start | bytes 1216512 | tf_op jit(solution)/shard_map/all_gather | solution.py:90
  9.4 226.2 %all-gather.13.cloned.1.call-start = ((), (), s32[]{:S(2)}) async-start(), calls=%async_computation.9 | async-start | bytes 1216512 | tf_op jit(solution)/shard_map/all_gather | solution.py:95
  10.0 291.0 %all-gather.15.cloned.1.call-start = ((), (), s32[]{:S(2)}) async-start(), calls=%async_computation.10 | async-start | bytes 4866048 | tf_op jit(solution)/shard_map/all_gather | solution.py:101
  10.6 355.7 %all-gather.17.cloned.1.call-start = ((), (), s32[]{:S(2)}) async-start(), calls=%async_computation.11 | async-start | bytes 4866048 | tf_op jit(solution)/shard_map/all_gather | solution.py:103
  11.1 550.3 %reduce-scatter.13.cloned.1.call-start = ((), (), s32[]{:S(2)}) async-start(), calls=%async_computation.12 | async-start | bytes 2433024 | tf_op jit(solution)/shard_map/reduce_scatter | solution.py:238
  61.2 62.8 %copy-start.30 = (bf16[4,1,160,768]{3,2,1,0:T(8,128)(2,1)S(1)}, bf16[4,1,160,768]{3,2,1,0:T(8,128)(2,1)}, u32[]{:S(2)}) copy-start(bf16[4,1,160,768]{3,2,1,0:T(8,128)(2,1)} %param.18) | copy-start | bytes 2949124
  70.4 57.0 %copy-start.28 = (s32[4,2,160]{2,1,0:T(2,128)S(1)}, s32[4,2,160]{2,1,0:T(2,128)}, u32[]{:S(2)}) copy-start(s32[4,2,160]{2,1,0:T(2,128)} %param.19) | copy-start | bytes 15364
  70.4 113.2 %collective-permute-start.1 = (bf16[4,160,768]{2,1,0:T(8,128)(2,1)S(1)}, bf16[4,160,768]{2,1,0:T(8,128)(2,1)}, u32[]{:S(2)}, u32[]{:S(2)}) collective-permute-start(bf16[4,160,768]{2,1,0:T(8,128)(2,1)S(1)} %convolution_convert_fusion.2), channel_id=1, source_target_pairs={{0,1},{1,0},{2,3},{3,2},{4,5},{5,4},{6,7},{7,6},{8,9},{9,8},{10,11... | collective-permute-start | bytes 2949128 | tf_op jit(solution)/shard_map/ppermute | solution.py:14
  127.1 60.3 %collective-permute-start = (bf16[4,160,768]{2,1,0:T(8,128)(2,1)}, bf16[4,160,768]{2,1,0:T(8,128)(2,1)}, u32[]{:S(2)}, u32[]{:S(2)}) collective-permute-start(bf16[4,160,768]{2,1,0:T(8,128)(2,1)} %add_convert_fusion.5), channel_id=1, source_target_pairs={{0,1},{1,0},{2,3},{3,2},{4,5},{5,4},{6,7},{7,6},{8,9},{9,8},{10,11... | collective-permute-start | bytes 2949128 | tf_op jit(solution)/shard_map/ppermute | solution.py:14
  127.5 252.5 %copy-start.26 = (f32[3072]{0:T(1024)}, f32[3072]{0:T(1024)S(1)}, u32[]{:S(2)}) copy-start(f32[3072]{0:T(1024)S(1)} %convert_element_type.144) | copy-start | bytes 36868
  196.9 4.5 copy-start
  238.8 154.5 %copy-start.8 = (f32[4,160,768]{2,1,0:T(8,128)}, f32[4,160,768]{2,1,0:T(8,128)S(1)}, u32[]{:S(2)}) copy-start(f32[4,160,768]{2,1,0:T(8,128)S(1)} %get-tuple-element.109) | copy-start | bytes 5898244
  308.8 66.4 %copy-start.10 = (bf16[4,1,160,768]{3,2,1,0:T(8,128)(2,1)S(1)}, bf16[4,1,160,768]{3,2,1,0:T(8,128)(2,1)}, u32[]{:S(2)}) copy-start(bf16[4,1,160,768]{3,2,1,0:T(8,128)(2,1)} %param.35) | copy-start | bytes 2949124
  366.2 13.8 %copy-start.34 = (f32[4,160,3072]{2,1,0:T(8,128)S(1)}, f32[4,160,3072]{2,1,0:T(8,128)}, u32[]{:S(2)}) copy-start(f32[4,160,3072]{2,1,0:T(8,128)} %fusion.15) | copy-start | bytes 23592964
  375.2 4.8 slice-start.5
  376.0 4.1 slice-start.6
  377.7 11.0 %slice-start.3 = ((s8[4718592]{0:T(1024)(128)(4,1)}), s8[4194304]{0:T(1024)(128)(4,1)S(1)}, s32[]{:S(2)}) async-start(s8[4718592]{0:T(1024)(128)(4,1)} %bitcast.190), calls=%async_computation.21 | async-start | bytes 8388608
  380.0 8.7 copy-start.18
  380.1 8.6 slice-start.4
  388.7 4.6 copy-start.15
  394.1 2.1 copy-start.33
  394.1 4.8 copy-start.20
  396.2 2.6 copy-start.29
  402.4 202.8 %reduce-scatter.19.cloned.1.call-start = ((), (), s32[]{:S(2)}) async-start(), calls=%async_computation.15 | async-start | bytes 2433024
  402.4 12.0 %slice-start = ((s8[11796480]{0:T(1024)(128)(4,1)}), s8[4194304]{0:T(1024)(128)(4,1)S(1)}, s32[]{:S(2)}) async-start(s8[11796480]{0:T(1024)(128)(4,1)} %bitcast.169), calls=%async_computation.18 | async-start | bytes 8388608
  402.4 12.0 %slice-start.1 = ((s8[11796480]{0:T(1024)(128)(4,1)}), s8[4194304]{0:T(1024)(128)(4,1)S(1)}, s32[]{:S(2)}) async-start(s8[11796480]{0:T(1024)(128)(4,1)} %bitcast.169), calls=%async_computation.19 | async-start | bytes 8388608
  402.4 12.0 %slice-start.2 = ((s8[11796480]{0:T(1024)(128)(4,1)}), s8[3407872]{0:T(1024)(128)(4,1)S(1)}, s32[]{:S(2)}) async-start(s8[11796480]{0:T(1024)(128)(4,1)} %bitcast.169), calls=%async_computation.20 | async-start | bytes 6815744
  414.4 6.9 copy-start.2
  421.3 3.3 copy-start.1
  438.0 271.1 %reduce-scatter.23.cloned.1.call-start = ((), (), s32[]{:S(2)}) async-start(), calls=%async_computation.17 | async-start | bytes 2433024
  445.0 2.2 copy-start.4
  449.1 4.5 collective-permute-start.3
  453.7 3.7 copy-start.31
  460.5 353.2 %reduce-scatter.21.cloned.1.call-start = ((), (), s32[]{:S(2)}) async-start(), calls=%async_computation.16 | async-start | bytes 2433024
  465.8 2.1 copy-start.5
  469.9 4.4 collective-permute-start.2
  474.4 2.1 copy-start.32
  479.6 475.0 %reduce-scatter.17.cloned.1.call-start = ((), (), s32[]{:S(2)}) async-start(), calls=%async_computation.14 | async-start | bytes 9732096 | tf_op jit(solution)/shard_map/reduce_scatter | solution.py:175
  493.0 603.5 %reduce-scatter.15.cloned.1.call-start = ((), (), s32[]{:S(2)}) async-start(), calls=%async_computation.13 | async-start | bytes 9732096 | tf_op jit(solution)/shard_map/reduce_scatter | solution.py:173
  505.2 4.2 copy-start.23
  505.2 4.2 copy-start.24
  505.2 4.2 copy-start.25
  505.2 52.8 %copy-start.17 = (bf16[4,160,768]{2,1,0:T(8,128)(2,1)S(1)}, bf16[4,160,768]{2,1,0:T(8,128)(2,1)}, u32[]{:S(2)}) copy-start(bf16[4,160,768]{2,1,0:T(8,128)(2,1)} %copy-done.16) | copy-start | bytes 2949124
  555.6 2.4 copy-start.7
  555.6 2.5 copy-start.14
  555.6 2.5 copy-start.21
  (10 other events, 13.4 us)
Sparse Core Ops, SparseCore 0:
  10.9 56.9 all-gather.10
  70.8 53.1 all-gather.6
  126.9 52.9 all-gather.8
  182.6 52.9 all-gather.12
  238.4 62.5 all-gather.14
  303.8 62.4 all-gather.16
  402.5 97.8 reduce-scatter.12
  507.0 98.0 reduce-scatter.18
  611.0 97.9 reduce-scatter.22
  715.6 98.0 reduce-scatter.20
  820.1 134.4 reduce-scatter.16
  962.0 134.4 reduce-scatter.14
where the time goes:
time: 1110 us; the launch traced here: 1100 us
  waiting for transfers between devices  798 us (72%)
  matrix products  119 us (11%)
  blocking collectives  83.4 us (8%)
  local copies, waits for them, and re-layouts  59.1 us (5%)
  other arithmetic  26.4 us (2%)
  between operations  15.2 us (1%)
    unnamed x15, waiting for transfers between devices  256 us
    reduce_scatter x1, waiting for transfers between devices, local(): lax.psum_scatter(feedforward_terms[0], ('batch', 'pair'), scatter_dimensi...  142 us
    reduce_scatter x1, waiting for transfers between devices, local(): lax.psum_scatter(feedforward_terms[2], ('batch', 'pair'), scatter_dimensi...  141 us
    unnamed x2, blocking collectives  83.4 us
    all_gather x1, waiting for transfers between devices, local(): lax.all_gather(feedforward_shards[0], ('batch', 'pair'), axis=0, tiled=True)  61.8 us
    all_gather x1, waiting for transfers between devices, local(): lax.all_gather(feedforward_shards[2], ('batch', 'pair'), axis=0, tiled=True)  57.4 us
    all_gather x1, waiting for transfers between devices, local(): lax.all_gather(attention_shards[3], ('batch', 'pair'), axis=0, tiled=True)  53.2 us
    all_gather x1, waiting for transfers between devices, local(): lax.all_gather(attention_shards[0], ('batch', 'pair'), axis=0, tiled=True)  52.1 us
  transfers between devices with their start and end apart: 16, of which 11 were waited for; matrix products, arithmetic and copies ran while one was open for 14% of the time, Pallas kernels for 0%

commit v1 on v0

--- a/solution.py
+++ b/solution.py
@@ -1,8 +1,11 @@
 import jax
 import jax.numpy as jnp
 from jax import lax
+from jax.experimental import pallas as pl
+from jax.experimental.pallas import tpu as pltpu
 from jax.sharding import PartitionSpec as P
 
+BATCH, PAIR = AXES = ("batch", "pair")
 HEAD_DIM = 64
 
 
@@ -87,23 +90,23 @@
     )
     feedforward_shards = (up_weight, up_bias, down_weight, down_bias, second_gain, second_shift)
     attention_full = (
-        lax.all_gather(attention_shards[0], ("batch", "pair"), axis=0, tiled=True),
-        lax.all_gather(attention_shards[1], ("batch", "pair"), axis=0, tiled=True),
-        lax.all_gather(attention_shards[2], ("batch", "pair"), axis=0, tiled=True),
-        lax.all_gather(attention_shards[3], ("batch", "pair"), axis=0, tiled=True),
-        lax.all_gather(attention_shards[4], ("batch", "pair"), axis=0, tiled=True),
-        lax.all_gather(attention_shards[5], ("batch", "pair"), axis=0, tiled=True),
-        lax.all_gather(attention_shards[6], ("batch", "pair"), axis=0, tiled=True),
-        lax.all_gather(attention_shards[7], ("batch", "pair"), axis=0, tiled=True),
-        lax.all_gather(attention_shards[8], ("batch", "pair"), axis=0, tiled=True),
+        lax.all_gather(attention_shards[0], AXES, axis=0, tiled=True),
+        lax.all_gather(attention_shards[1], AXES, axis=0, tiled=True),
+        lax.all_gather(attention_shards[2], AXES, axis=0, tiled=True),
+        lax.all_gather(attention_shards[3], AXES, axis=0, tiled=True),
+        lax.all_gather(attention_shards[4], AXES, axis=0, tiled=True),
+        lax.all_gather(attention_shards[5], AXES, axis=0, tiled=True),
+        lax.all_gather(attention_shards[6], AXES, axis=0, tiled=True),
+        lax.all_gather(attention_shards[7], AXES, axis=0, tiled=True),
+        lax.all_gather(attention_shards[8], AXES, axis=0, tiled=True),
     )
     feedforward_full = (
-        lax.all_gather(feedforward_shards[0], ("batch", "pair"), axis=0, tiled=True),
-        lax.all_gather(feedforward_shards[1], ("batch", "pair"), axis=0, tiled=True),
-        lax.all_gather(feedforward_shards[2], ("batch", "pair"), axis=0, tiled=True),
-        lax.all_gather(feedforward_shards[3], ("batch", "pair"), axis=0, tiled=True),
-        lax.all_gather(feedforward_shards[4], ("batch", "pair"), axis=0, tiled=True),
-        lax.all_gather(feedforward_shards[5], ("batch", "pair"), axis=0, tiled=True),
+        lax.all_gather(feedforward_shards[0], AXES, axis=0, tiled=True),
+        lax.all_gather(feedforward_shards[1], AXES, axis=0, tiled=True),
+        lax.all_gather(feedforward_shards[2], AXES, axis=0, tiled=True),
+        lax.all_gather(feedforward_shards[3], AXES, axis=0, tiled=True),
+        lax.all_gather(feedforward_shards[4], AXES, axis=0, tiled=True),
+        lax.all_gather(feedforward_shards[5], AXES, axis=0, tiled=True),
     )
     (
         query_mat,
@@ -117,7 +120,7 @@
         shift_first,
     ) = attention_full
     up_mat, up_vec, down_mat, down_vec, gain_second, shift_second = feedforward_full
-    pair_index = lax.axis_index("pair")
+    pair_index = lax.axis_index(PAIR)
     own_ids = lax.dynamic_index_in_dim(segment_ids, pair_index, 1, keepdims=False)
     other_ids = lax.dynamic_index_in_dim(segment_ids, 1 - pair_index, 1, keepdims=False)
     key_ids = jnp.concatenate([own_ids, other_ids], 1)
@@ -125,7 +128,7 @@
     queries = (matmul(token_rows, query_mat) + query_vec).astype(jnp.bfloat16)
     keys_own = matmul(token_rows, key_mat).astype(jnp.bfloat16)
     values_own = (matmul(token_rows, value_mat) + value_vec).astype(jnp.bfloat16)
-    keys_other, values_other = swapped((keys_own, values_own), "pair", 0)
+    keys_other, values_other = swapped((keys_own, values_own), PAIR, 0)
     head_rows = (seqs, 2 * slots, heads, HEAD_DIM)
     key_rows = jnp.concatenate([keys_own, keys_other], 1).reshape(head_rows)
     value_rows = jnp.concatenate([values_own, values_other], 1).reshape(head_rows)
@@ -170,12 +173,12 @@
         shift_second_grad,
     )
     feedforward_parts = (
-        lax.psum_scatter(feedforward_terms[0], ("batch", "pair"), scatter_dimension=0, tiled=True),
-        lax.psum_scatter(feedforward_terms[1], ("batch", "pair"), scatter_dimension=0, tiled=True),
-        lax.psum_scatter(feedforward_terms[2], ("batch", "pair"), scatter_dimension=0, tiled=True),
-        lax.psum_scatter(feedforward_terms[3], ("batch", "pair"), scatter_dimension=0, tiled=True),
-        lax.psum_scatter(feedforward_terms[4], ("batch", "pair"), scatter_dimension=0, tiled=True),
-        lax.psum_scatter(feedforward_terms[5], ("batch", "pair"), scatter_dimension=0, tiled=True),
+        lax.psum_scatter(feedforward_terms[0], AXES, scatter_dimension=0, tiled=True),
+        lax.psum_scatter(feedforward_terms[1], AXES, scatter_dimension=0, tiled=True),
+        lax.psum_scatter(feedforward_terms[2], AXES, scatter_dimension=0, tiled=True),
+        lax.psum_scatter(feedforward_terms[3], AXES, scatter_dimension=0, tiled=True),
+        lax.psum_scatter(feedforward_terms[4], AXES, scatter_dimension=0, tiled=True),
+        lax.psum_scatter(feedforward_terms[5], AXES, scatter_dimension=0, tiled=True),
     )
     branch_low = first_grad.astype(jnp.bfloat16)
     out_weight_grad = outer_sum(mixed, branch_low)
@@ -205,8 +208,8 @@
     )
     value_grad_all = value_grad_all.reshape(seqs, 2 * slots, width)
     keys_back, values_back = (
-        swapped(key_grad_all[:, slots:].astype(jnp.bfloat16), "pair", 0).astype(jnp.float32),
-        swapped(value_grad_all[:, slots:].astype(jnp.bfloat16), "pair", 0).astype(jnp.float32),
+        swapped(key_grad_all[:, slots:].astype(jnp.bfloat16), PAIR, 0).astype(jnp.float32),
+        swapped(value_grad_all[:, slots:].astype(jnp.bfloat16), PAIR, 0).astype(jnp.float32),
     )
     key_grad = (key_grad_all[:, :slots] + keys_back).astype(jnp.bfloat16)
     value_grad = (value_grad_all[:, :slots] + values_back).astype(jnp.bfloat16)
@@ -230,15 +233,15 @@
         shift_first_grad,
     )
     attention_parts = (
-        lax.psum_scatter(attention_terms[0], ("batch", "pair"), scatter_dimension=0, tiled=True),
-        lax.psum_scatter(attention_terms[1], ("batch", "pair"), scatter_dimension=0, tiled=True),
-        lax.psum_scatter(attention_terms[2], ("batch", "pair"), scatter_dimension=0, tiled=True),
-        lax.psum_scatter(attention_terms[3], ("batch", "pair"), scatter_dimension=0, tiled=True),
-        lax.psum_scatter(attention_terms[4], ("batch", "pair"), scatter_dimension=0, tiled=True),
-        lax.psum_scatter(attention_terms[5], ("batch", "pair"), scatter_dimension=0, tiled=True),
-        lax.psum_scatter(attention_terms[6], ("batch", "pair"), scatter_dimension=0, tiled=True),
-        lax.psum_scatter(attention_terms[7], ("batch", "pair"), scatter_dimension=0, tiled=True),
-        lax.psum_scatter(attention_terms[8], ("batch", "pair"), scatter_dimension=0, tiled=True),
+        lax.psum_scatter(attention_terms[0], AXES, scatter_dimension=0, tiled=True),
+        lax.psum_scatter(attention_terms[1], AXES, scatter_dimension=0, tiled=True),
+        lax.psum_scatter(attention_terms[2], AXES, scatter_dimension=0, tiled=True),
+        lax.psum_scatter(attention_terms[3], AXES, scatter_dimension=0, tiled=True),
+        lax.psum_scatter(attention_terms[4], AXES, scatter_dimension=0, tiled=True),
+        lax.psum_scatter(attention_terms[5], AXES, scatter_dimension=0, tiled=True),
+        lax.psum_scatter(attention_terms[6], AXES, scatter_dimension=0, tiled=True),
+        lax.psum_scatter(attention_terms[7], AXES, scatter_dimension=0, tiled=True),
+        lax.psum_scatter(attention_terms[8], AXES, scatter_dimension=0, tiled=True),
     )
     return (
         layer_output,
@@ -261,44 +264,1498 @@
     )
 
 
+F32 = jnp.float32
+BF16 = jnp.bfloat16
+MESH = pl.DeviceIdType.MESH
+CHIPS = 16
+LINE = 4
+VMEM_BYTES = 63 * 1024 * 1024
+
+
+def dot(left, right, left_dim, right_dim, precision=None):
+    return lax.dot_general(
+        left,
+        right,
+        (((left_dim,), (right_dim,)), ((), ())),
+        preferred_element_type=F32,
+        precision=precision,
+    )
+
+
+def nn(left, right):
+    return dot(left, right, 1, 0)
+
+
+def nt(left, right):
+    return dot(left, right, 1, 1)
+
+
+def tn(left, right):
+    return dot(left, right, 0, 0)
+
+
+def iota(shape, dim):
+    return lax.broadcasted_iota(jnp.int32, shape, dim)
+
+
+class Refs(dict):
+    __getattr__ = dict.__getitem__
+    __setattr__ = dict.__setitem__
+
+
+def column_sum(values):
+    return jnp.sum(values, 0, keepdims=True)
+
+
+def lane_mean(values):
+    return jnp.mean(values, -1, keepdims=True)
+
+
+def block(start, size):
+    return pl.ds(pl.multiple_of(start * size, size), size)
+
+
+def each(count, act):
+    def step(s, carry):
+        act(s)
+        return carry
+
+    lax.fori_loop(0, count, step, 0)
+
+
+class Links:
+    def __init__(self):
+        self.b = lax.axis_index(BATCH)
+        self.p = lax.axis_index(PAIR)
+        self.z = lax.div(self.b, 4)
+        x = lax.rem(self.b, 2)
+        y = lax.rem(lax.div(self.b, 2), 2)
+        self.f = x + self.p * (y - x)
+        self.g = y + self.p * (x - y)
+        self.near = self.chip(self.z, 1)
+        self.far = self.index(self.z, self.f, 1 - self.g)
+        third = lax.div(self.z, 3)
+        second = lax.div(self.z, 2) - third
+        zeroth = 1 - lax.div(self.z + 3, 4)
+        self.is_z = (zeroth, 1 - zeroth - second - third, second, third)
+
+    def index(self, z, f, g):
+        return 4 * z + (1 + self.p) * f + (2 - self.p) * g
+
+    def chip(self, z, side):
+        return self.index(z, self.f + side * (1 - 2 * self.f), self.g)
+
+    def by_z(self, values):
+        return sum(flag * value for flag, value in zip(self.is_z, values))
+
+    def column(self):
+        return [lax.rem(self.z + step, LINE) for step in (1, 3, 2)]
+
+    def other(self):
+        return (self.b, 1 - self.p)
+
+    def greet(self):
+        semaphore = pltpu.get_barrier_semaphore()
+        partners = [self.chip(z, 0) for z in self.column()] + [self.near, self.far]
+        for device in [(chip, self.p) for chip in partners] + [self.other()]:
+            pl.semaphore_signal(semaphore, inc=1, device_id=device, device_id_type=MESH)
+
+    def meet(self):
+        pl.semaphore_wait(pltpu.get_barrier_semaphore(), 6)
+
+
+class Gather:
+    ARRIVE = ((1, 2, 3), (2, 0, 3), (3, 1, 0), (2, 1, 0))
+    FROM_FAR = CHIPS
+    ARRIVALS = CHIPS + 1
+
+    def __init__(self, links, ref, send, recv, near_first=False):
+        self.links, self.ref, self.send, self.recv = links, ref, send, recv
+        self.size = ref.shape[0] // CHIPS
+        self.near_first = near_first
+
+    def copy(self, rows, chip, arrival):
+        part = self.ref.at[rows]
+        return pltpu.make_async_remote_copy(
+            src_ref=part,
+            dst_ref=part,
+            send_sem=self.send,
+            recv_sem=self.recv.at[arrival],
+            device_id=(chip, self.links.p),
+            device_id_type=MESH,
+        )
+
+    def wait(self, shard):
+        self.copy(block(shard, self.size), self.links.far, shard).wait_recv()
+
+    def to_far(self, z, side):
+        shard = self.links.chip(z, side)
+        self.copy(block(shard, self.size), self.links.far, self.FROM_FAR).start()
+
+    def to_near(self, z):
+        shard = self.links.chip(z, 0)
+        self.copy(block(shard, self.size), self.links.near, shard).start()
+
+    def to_column(self, z, side):
+        k = self.links
+        shard = k.chip(k.z, side)
+        self.copy(block(shard, self.size), k.chip(z, 0), shard).start()
+
+    def own(self):
+        k = self.links
+        self.to_near(k.z)
+        self.to_far(k.z, 0)
+        for z in k.column():
+            self.to_column(z, 0)
+
+    def near(self, turn):
+        k = self.links
+        z = k.z if turn == 0 else k.by_z([order[turn - 1] for order in self.ARRIVE])
+        self.wait(k.chip(z, 1))
+        if self.near_first and turn == 0:
+            for other in k.column():
+                self.to_column(other, 1)
+        self.to_far(z, 1)
+
+    def along(self, turn):
+        k = self.links
+        z = k.by_z([order[turn] for order in self.ARRIVE])
+        self.wait(k.chip(z, 0))
+        if not self.near_first:
+            self.to_near(z)
+        self.to_far(z, 0)
+
+    def steps(self):
+        steps = [self.own, lambda: self.near(0)]
+        for turn in range(LINE - 1):
+            steps.append(lambda turn=turn: self.along(turn))
+            steps.append(lambda turn=turn: self.near(turn + 1))
+        return steps
+
+    def finish(self):
+        self.copy(slice(0, 8 * self.size), self.links.far, self.FROM_FAR).wait_recv()
+
+    def drain(self):
+        self.copy(slice(0, 15 * self.size), self.links.far, self.FROM_FAR).wait_send()
+
+
+class Reduce:
+    LEAVE = ((3, 2, 1), (3, 2, 0), (0, 1, 3), (0, 1, 2))
+    SLOTS = 15
+    ARRIVALS = 10
+
+    def __init__(self, links, grad, land, send, recv, near_first=False):
+        self.links, self.grad, self.land = links, grad, land
+        self.send, self.recv = send, recv
+        self.size = grad.shape[0] // CHIPS
+        self.near_first = near_first
+
+    def rows(self, z, f, count=1, far=0):
+        k = self.links
+        g = k.g + far * (1 - 2 * k.g)
+        at = 4 * z + 2 * g + f
+        return pl.ds(pl.multiple_of(at * self.size, self.size), count * self.size)
+
+    def slots(self, slot, count=1):
+        start = slot * self.size
+        return pl.ds(start if isinstance(slot, int) else pl.multiple_of(start, self.size), count * self.size)
+
+    def copy(self, rows, slots, chip, arrival):
+        return pltpu.make_async_remote_copy(
+            src_ref=self.grad.at[rows],
+            dst_ref=self.land.at[slots],
+            send_sem=self.send,
+            recv_sem=self.recv.at[arrival],
+            device_id=(chip, self.links.p),
+            device_id_type=MESH,
+        )
+
+    def wait(self, arrival, count):
+        rows = slice(0, count * self.size)
+        self.copy(rows, rows, self.links.far, arrival).wait_recv()
+
+    def wait_far(self, z):
+        self.wait(z, 2)
+
+    def wait_near(self, z):
+        self.wait(4 if self.near_first else 4 + z, 1)
+
+    def wait_column(self, side):
+        self.wait(8 + side, 3)
+
+    def far_slot(self, z, f):
+        return 2 * z + f
+
+    def near_slot(self, z):
+        return 8 if self.near_first else 8 + z
+
+    def column_slot(self, step, side):
+        return (9 + 3 * side if self.near_first else 12) + step - 1
+
+    def column_slots(self, side):
+        return [self.column_slot(step, side) for step in range(1, LINE)]
+
+    def total(self, rows, slots):
+        total = self.grad[rows].astype(F32)
+        for slot in slots:
+            total = total + self.land[self.slots(slot)].astype(F32)
+        return total
+
+    def add_on(self, rows, slots):
+        self.grad[rows] = self.total(rows, slots).astype(self.grad.dtype)
+
+    def far(self, z):
+        self.copy(self.rows(z, 0, 2, 1), self.slots(self.far_slot(z, 0), 2), self.links.far, z).start()
+
+    def near(self, z):
+        k = self.links
+        more = []
+        self.wait_far(z)
+        if self.near_first:
+            self.wait_column(1)
+            more = self.column_slots(1)
+        rows = self.rows(z, 1 - k.f)
+        self.add_on(rows, [self.far_slot(z, 1 - k.f)] + more)
+        arrival = 4 if self.near_first else 4 + z
+        self.copy(rows, self.slots(self.near_slot(z)), k.near, arrival).start()
+
+    def along(self, turn, side):
+        k = self.links
+        z = k.by_z([order[turn] for order in self.LEAVE])
+        f = k.f + side * (1 - 2 * k.f)
+        rows, more = self.rows(z, f), []
+        if not self.near_first:
+            self.wait_near(z)
+            more = [self.near_slot(z)]
+        elif side == 1:
+            self.wait_far(z)
+        self.add_on(rows, [self.far_slot(z, f)] + more)
+        slot = self.column_slot(lax.rem(k.z - z + LINE, LINE), side)
+        self.copy(rows, self.slots(slot), k.chip(z, 0), 8 + side).start()
+
+    def steps(self):
+        steps = [lambda z=z: self.far(z) for z in range(LINE)]
+        near = [lambda z=z: self.near(z) for z in range(LINE)]
+        sides = (1, 0) if self.near_first else (0,)
+        along = [
+            lambda turn=turn, side=side: self.along(turn, side)
+            for turn in range(LINE - 1)
+            for side in sides
+        ]
+        if self.near_first:
+            return steps + along + [lambda: self.near(self.links.z)]
+        return steps + near + along
+
+    def result(self):
+        k = self.links
+        self.wait_near(k.z)
+        self.wait_column(0)
+        slots = [self.far_slot(k.z, k.f), self.near_slot(k.z)]
+        return self.total(self.rows(k.z, k.f), slots + self.column_slots(0))
+
+    def drain(self):
+        rows = slice(0, 15 * self.size)
+        self.copy(rows, rows, self.links.far, 0).wait_send()
+
+
+class Steps:
+    def __init__(self, seqs, course, transfers):
+        lines = [iter(steps) for steps in transfers]
+        self.seqs, self.count = seqs, 0
+        self.waiting = {place: [next(lines[n]) for n in order] for place, order in course.items()}
+        assert all(next(line, None) is None for line in lines)
+
+    def run(self):
+        for step in self.waiting.pop(self.count, ()):
+            step()
+        self.count += 1
+
+    def once(self, act):
+        self.run()
+        act()
+
+    def loop(self, act, first=None, count=None):
+        count = self.seqs if count is None else count
+        self.run()
+        if first is not None:
+            first()
+        later = []
+        for s in range(1, count):
+            later.append((s, self.waiting.pop(self.count, ())))
+            self.count += 1
+
+        def turn(s):
+            for at, steps in later:
+                if steps:
+
+                    @pl.when(s == at)
+                    def _():
+                        for step in steps:
+                            step()
+
+            act(s)
+
+        each(count, turn)
+
+
+def laying(blocks, cols):
+    size = cols // blocks
+    pick = iota((128, cols), 0) == lax.rem(iota((128, cols), 1), size)
+    return pick, lax.div(iota((blocks, cols), 1), size) == iota((blocks, cols), 0)
+
+
+def core_order(chip, p):
+    low = lax.rem(chip, 4)
+    step = (low == 1).astype(jnp.int32) - (low == 2).astype(jnp.int32)
+    return chip + p * step
+
+
+def vector_rows(shape, dim, vector, p):
+    device, row = iota(shape, dim), iota(shape, 1 - dim)
+    return row == 16 * core_order(lax.div(device, 2), p) + 2 * vector + lax.rem(device, 2)
+
+
+def unit_rows(shape, dim, which, p):
+    return iota(shape, 1 - dim) == 16 * core_order(iota(shape, dim), p) + which
+
+
+def unpack_small(r, p):
+    rows = CHIPS * 16
+    flat = r.small_all[...].astype(BF16)
+    pick, place = laying(2 * CHIPS, r.vec.shape[1])
+    for vector in range(8):
+        chosen = nn(vector_rows((2 * CHIPS, rows), 0, vector, 0).astype(BF16), flat[:, :128])
+        laid = nn(chosen.astype(BF16), pick.astype(BF16))
+        r.vec[vector : vector + 1] = column_sum(jnp.where(place, laid, 0.0))
+    pick, place = laying(CHIPS, r.upb.shape[1])
+    chosen = nn(unit_rows((CHIPS, rows), 0, p, 0).astype(BF16), flat[:, 128:])
+    laid = nn(chosen.astype(BF16), pick.astype(BF16))
+    r.upb[...] = column_sum(jnp.where(place, laid, 0.0))
+
+
+def pack_small(r, p):
+    rows, width = CHIPS * 16, r.gvec.shape[1]
+    for vector in range(2, 8):
+        r.gvec[vector : vector + 1] = column_sum(r.gacc[8 * vector : 8 * vector + 8])
+    row = iota((rows, 1), 0)
+    device = 2 * core_order(lax.div(row, 16), p) + lax.rem(row, 2)
+    chosen = lax.div(lax.rem(iota((rows, 8), 0), 16), 2) == iota((rows, 8), 1)
+    spread = nn(chosen.astype(BF16), r.gvec[...].astype(BF16))
+    place = device == lax.div(iota((1, width), 1), width // (2 * CHIPS))
+    pick, _ = laying(2 * CHIPS, width)
+    narrow = nt(jnp.where(place, spread, 0.0).astype(BF16), pick.astype(BF16))
+    pick, place = laying(CHIPS, r.upg.shape[1])
+    blocks = nt(jnp.where(place, r.upg[...], 0.0).astype(BF16), pick.astype(BF16))
+    wide = nn(unit_rows((rows, CHIPS), 1, p, p).astype(BF16), blocks.astype(BF16))
+    low = jnp.concatenate([narrow, wide], 1).astype(BF16)
+    space = r.gq2.shape[0] // CHIPS
+    for chip in range(CHIPS):
+        r.gq2[space * chip + space - 16 : space * chip + space] = low[16 * chip : 16 * chip + 16]
+
+
+def half_lanes(values, half, factor=None):
+    mask = lax.div(iota((1, values.shape[1]), 1), HEAD_DIM) == half
+    kept = jnp.where(mask, values, jnp.zeros_like(values))
+    return kept if factor is None else kept * jnp.asarray(factor, values.dtype)
+
+
+def normalize(values):
+    centred = values - lane_mean(values)
+    scale = lax.rsqrt(lane_mean(centred * centred) + EPSILON)
+    return centred * scale, scale
+
+
+def norm_back(grad, hat, scale):
+    return scale * (grad - lane_mean(grad) - hat * lane_mean(grad * hat))
+
+
+def gelu_both(value):
+    square = value * value
+    root = 0.7978845608028654
+    inner = value * (root + root * 0.044715 * square)
+    bent = 0.5 * jnp.tanh(inner) + 0.5
+    slope = root + 3.0 * root * 0.044715 * square
+    return value * bent, bent + 2.0 * value * slope * (bent - bent * bent)
+
+
+UP_LANES = (slice(0, 768), slice(768, 1536),)
+UP_NEAR_FIRST = (False, True)
+DOWN_LANES = (slice(0, 512), slice(512, 768),)
+DOWN_NEAR_FIRST = (False, True)
+UP_SUM_LANES = (slice(0, 768), slice(768, 1536),)
+UP_SUM_NEAR_FIRST = (True, False)
+DOWN_SUM_LANES = (slice(0, 512), slice(512, 768),)
+DOWN_SUM_NEAR_FIRST = (False, True)
+UNITS = (
+    ("unpack",),
+    ("att", 0),
+    ("att", 1),
+    ("att", 2),
+    ("wo",),
+    ("out",),
+    ("up", 0),
+    ("up", 1),
+    ("do", 0),
+    ("dw", 0),
+    ("do", 1),
+    ("dw", 1),
+    ("ln2",),
+    ("ddw",),
+    ("gd", 0),
+    ("gd", 1),
+    ("gd", 2),
+    ("gd", 3),
+    ("hb",),
+    ("gu", 0),
+    ("gu", 1),
+    ("gu", 2),
+    ("gu", 3),
+    ("no",),
+    ("nw",),
+    ("ln1",),
+    ("mb",),
+    ("go",),
+    ("ab", 0),
+    ("gq", 0),
+    ("ab", 1),
+    ("gq", 1),
+    ("ab", 2),
+    ("ps",),
+    ("gq", 2),
+    ("to",),
+    ("tw",),
+    ("te",),
+    ("end",),
+)
+COURSE = {
+    0: (0, 1, 2, 3, 0, 0, 2, 4, 0, 0, 3, 1, 1, 6, 2, 1, 0, 0, 1, 3, 0, 1, 1, 5, 1, 2, 2, 3, 3,),
+    1: (2, 4, 2,),
+    2: (4,),
+    3: (2, 3, 3,),
+    4: (4, 4, 5,),
+    6: (6, 3,),
+    7: (6,),
+    8: (4, 4, 7,),
+    10: (6,),
+    12: (6, 5,),
+    15: (4,),
+    16: (5, 5,),
+    17: (5, 5, 6,),
+    18: (5, 6, 7, 7,),
+    23: (6,),
+    24: (7, 7,),
+    25: (7, 7, 7,),
+    40: (9,),
+    41: (9,),
+    42: (9,),
+    43: (9,),
+    44: (8,),
+    45: (8, 8, 8, 9,),
+    48: (9,),
+    49: (9, 9, 9, 8,),
+    50: (8, 8,),
+    52: (8, 10, 10, 10,),
+    55: (8, 9,),
+    59: (10, 11,),
+    60: (11, 8,),
+    63: (8, 11, 11,),
+    65: (10,),
+    67: (10, 11, 10, 10, 10, 10, 11,),
+    68: (11,),
+    69: (12, 11,),
+    70: (12,),
+    72: (12, 12, 12,),
+    74: (11,),
+    75: (12, 12, 12, 13, 11,),
+    77: (11, 13, 13, 13,),
+    79: (12, 12, 12, 13,),
+    80: (14, 13,),
+    81: (13, 13, 14, 14, 8, 14,),
+    83: (9, 13, 13, 13, 14, 14,),
+    85: (14, 14, 14, 14, 14, 12, 10,),
+    86: (9, 11, 10, 13, 14,),
+}
+
+
+class Layer:
+    def __init__(self, r, p):
+        self.r, self.p = r, p
+        self.slots = r.tokens.shape[2]
+        self.width = r.tokens.shape[3]
+        self.half = self.width // 2
+        self.units = r.wup.shape[1]
+
+    def rows(self, s):
+        return block(s, 2 * self.slots)
+
+    def side(self, s, side):
+        return block(2 * s + side, self.slots)
+
+    def own_lanes(self, pair):
+        return pl.ds(pl.multiple_of(self.p * self.half + 128 * pair, 128), 128)
+
+    def project(self, s, pair):
+        r = self.r
+        result = nn(r.x_all[self.rows(s)], r.wq[pair][...])
+        lanes = self.own_lanes(pair)
+        query = result[:, :128] + r.vec[0:1, lanes]
+        value = result[:, 256:] + r.vec[1:2, lanes]
+        r.qkv[pair, self.rows(s)] = jnp.concatenate([query, result[:, 128:256], value], 1).astype(BF16)
+
+    def mask(self, s):
+        r = self.r
+        rows, space = r.fill.shape[1:]
+        rest = jnp.zeros((1, space - rows), F32)
+        ids = [r.segment_ids[s, half : half + 1].astype(F32) for half in range(2)]
+        across = jnp.broadcast_to(jnp.concatenate(ids + [rest], 1), (space, space))
+        r.fill[s] = jnp.where(across.T[:rows] == across[:rows], 0.0, NEG_FILL).astype(BF16)
+
+    def heads(self, s, pair):
+        held = self.r.qkv[pair, self.rows(s)]
+        return held[:, :128], held[:, 128:256], held[:, 256:]
+
+    def widened(self, values):
+        rest = self.r.fill.shape[2] - values.shape[0]
+        return jnp.concatenate([values, jnp.zeros((rest, values.shape[1]), values.dtype)], 0)
+
+    def both_halves(self, values, factor=None, widen=False):
+        parts = [half_lanes(values, half, factor) for half in range(2)]
+        return jnp.concatenate([self.widened(part) if widen else part for part in parts], 0)
+
+    def attend(self, s, pair):
+        r = self.r
+        rows, space = r.fill.shape[1:]
+        queries, keys, values = self.heads(s, pair)
+        values_t = values.T
+        r.probs_grad[...] = nt(self.both_halves(keys, HEAD_DIM**-0.5), self.widened(queries))
+        parts = []
+        for half in range(2):
+            top, total = NEG_FILL, 0.0
+            for at in range(0, rows, 64):
+                here = slice(rows * half + at, rows * half + at + 64)
+                scores = r.probs_grad[here] + r.fill[s, at : at + 64].astype(F32)
+                r.probs_grad[here] = scores
+                top = jnp.maximum(top, jnp.max(scores.reshape(8, 8, space), 0))
+            top = jnp.max(top, 0, keepdims=True)
+            for at in range(0, rows, 64):
+                here = slice(rows * half + at, rows * half + at + 64)
+                raised = jnp.exp(r.probs_grad[here] - top)
+                r.probs_grad[here] = raised
+                total = total + jnp.sum(raised.reshape(8, 8, space), 0)
+            share = 1.0 / column_sum(total)
+            lanes = slice(space * half, space * half + space)
+            for at in range(0, rows, 64):
+                here = slice(rows * half + at, rows * half + at + 64)
+                r.pt[3 * s + pair, at : at + 64, lanes] = (r.probs_grad[here] * share).astype(BF16)
+            head = values_t[HEAD_DIM * half : HEAD_DIM * half + HEAD_DIM]
+            parts.append(nn(head, r.pt[3 * s + pair, :, lanes]))
+        mixed = jnp.concatenate(parts, 0).T[:rows]
+        r.mixed[self.rows(s), self.own_lanes(pair)] = mixed.astype(BF16)
+
+    def out_project(self, s):
+        r, p = self.r, self.p
+        mixed = r.mixed[self.side(s, p)]
+        sides = [nn(mixed, r.wo[side]) for side in range(2)]
+        r.product[: self.slots] = jnp.concatenate(sides, 1)
+        for at, rows in self.pieces(s):
+            resid = r.x_all[rows].astype(F32) + r.product[at] + r.vec[2:3]
+            hat, scale = normalize(resid)
+            r.xhat[s, at] = hat
+            r.rstd[s, at] = jnp.broadcast_to(scale, (scale.shape[0], 128))
+            r.n_all[rows] = (hat * r.vec[3:4] + r.vec[4:5]).astype(BF16)
+
+    def feed_up(self, s, lanes):
+        r = self.r
+        r.product[...] = nn(r.n_all[self.rows(s)], r.wup[:, lanes])
+        for at, rows in self.strips(s):
+            hidden, slope = gelu_both(r.product[at] + r.upb[:, lanes])
+            r.hidden[rows, lanes] = hidden.astype(BF16)
+            r.slope[rows, lanes] = slope.astype(BF16)
+
+    def two(self, ref, n, side):
+        return jnp.concatenate([ref[self.side(2 * n + s, side)] for s in range(2)], 0)
+
+    def by_two(self, rows):
+        return rows.reshape(2, self.slots, rows.shape[1])
+
+    def feed_down(self, n, side, lanes):
+        return self.by_two(nn(self.two(self.r.hidden, n, side), self.r.wdown[:, lanes]))
+
+    def pieces(self, s):
+        for at in range(0, self.slots, 32):
+            start = (2 * s + self.p) * self.slots + at
+            yield slice(at, at + 32), pl.ds(pl.multiple_of(start, 32), 32)
+
+    def strips(self, s):
+        for at in range(0, 2 * self.slots, 32):
+            start = 2 * s * self.slots + at
+            yield slice(at, at + 32), pl.ds(pl.multiple_of(start, 32), 32)
+
+    def add_rows(self, vector, values):
+        folded = values.reshape(values.shape[0] // 8, 8, values.shape[1])
+        self.r.gacc[8 * vector : 8 * vector + 8] += jnp.sum(folded, 0)
+
+    def finish_norm(self, s):
+        r = self.r
+        for at, rows in self.pieces(s):
+            normed = r.xhat[s, at] * r.vec[3:4] + r.vec[4:5]
+            resid = normed + r.part_own[s, at] + r.part_in[s, at].astype(F32) + r.vec[5:6]
+            hat, scale = normalize(resid)
+            r.final[s, at] = (hat * r.vec[6:7] + r.vec[7:8]).astype(BF16)
+            grad = r.out_grad[s, at].astype(F32)
+            self.add_rows(6, grad * hat)
+            self.add_rows(7, grad)
+            back = norm_back(grad * r.vec[6:7], hat, scale)
+            r.resid_grad[s, at] = back
+            low = back.astype(BF16)
+            r.dd_all[rows] = low
+            self.add_rows(5, low.astype(F32))
+
+    def put_blocks(self, ref, first, result, size):
+        space = ref.shape[0] // CHIPS
+        low = result.astype(BF16)
+        for n in range(result.shape[0] // size):
+            chip = first + n
+            step = (0, 1, -1, 0)[chip % 4]
+            at = chip * space
+            rows = pl.ds(pl.multiple_of(at + self.p * step * space, 16), size) if step else slice(at, at + size)
+            ref[rows] = low[n * size : n * size + size]
+
+    def down_weight_grad(self, m):
+        r = self.r
+        at = slice(self.half * m, self.half * m + self.half)
+        self.put_blocks(r.gd, 4 * m, tn(r.hidden[:, at], r.dd_all[...]), self.half // 4)
+
+    def hidden_back(self, s):
+        r = self.r
+        grads = r.dd_all[self.rows(s)]
+        for start in range(0, self.units, self.width):
+            lanes = slice(start, start + self.width)
+            r.product[...] = nt(grads, r.wdown[lanes])
+            total = 0.0
+            for at, rows in self.strips(s):
+                low = (r.product[at] * r.slope[rows, lanes].astype(F32)).astype(BF16)
+                r.slope[rows, lanes] = low
+                total = total + jnp.sum(low.astype(F32).reshape(4, 8, self.width), 0)
+            r.upg[:, lanes] += column_sum(total)
+
+    def up_weight_grad(self, m, n):
+        r = self.r
+        at = slice(self.half * m, self.half * m + self.half)
+        lanes = slice(self.width * n, self.width * n + self.width)
+        self.put_blocks(r.gu.at[:, lanes], 8 * m, tn(r.n_all[:, at], r.slope[:, lanes]), self.half // 8)
+
+    def normed_back(self, n, side):
+        return self.by_two(nt(self.two(self.r.slope, n, side), self.r.wup[...]))
+
+    def first_norm_back(self, s):
+        r = self.r
+        for at, rows in self.pieces(s):
+            grad = r.part_own[s, at] + r.part_in[s, at].astype(F32) + r.resid_grad[s, at]
+            hat = r.xhat[s, at]
+            self.add_rows(3, grad * hat)
+            self.add_rows(4, grad)
+            back = norm_back(grad * r.vec[3:4], hat, r.rstd[s, at, 0:1])
+            r.resid_grad[s, at] = back
+            low = back.astype(BF16)
+            r.n_all[rows] = low
+            self.add_rows(2, low.astype(F32))
+
+    def out_weight_grad(self):
+        r = self.r
+        own = block(self.p, self.half)
+        right = r.n_all[:, own]
+        for m in range(2):
+            at = slice(self.half * m, self.half * m + self.half)
+            self.put_blocks(r.go, 8 * m, tn(r.mixed[:, at], right), self.half // 8)
+
+    def mixed_back(self, s):
+        r = self.r
+        grads = r.n_all[self.rows(s)]
+        own = block(self.p, self.half)
+        total = nt(grads[:, : self.half], r.wo[0, own]) + nt(grads[:, self.half :], r.wo[1, own])
+        r.dm[self.rows(s)] = total.astype(BF16)
+
+    def attend_back(self, s, pair):
+        r = self.r
+        scale = HEAD_DIM**-0.5
+        unit = 3 * s + pair
+        rows, space = r.fill.shape[1:]
+        queries, keys, values = self.heads(s, pair)
+        grads = r.dm[self.rows(s), 128 * pair : 128 * pair + 128]
+        r.probs_grad[...] = nt(self.both_halves(values), self.widened(grads))
+        for half in range(2):
+            lanes = slice(space * half, space * half + space)
+            total = 0.0
+            for at in range(0, rows, 64):
+                grad = r.probs_grad[rows * half + at : rows * half + at + 64]
+                product = r.pt[unit, at : at + 64, lanes].astype(F32) * grad
+                total = total + jnp.sum(product.reshape(8, 8, space), 0)
+            delta = column_sum(total)
+            for at in range(0, rows, 64):
+                grad = r.probs_grad[rows * half + at : rows * half + at + 64]
+                probs = r.pt[unit, at : at + 64, lanes].astype(F32)
+                r.score_grad[at : at + 64, lanes] = (probs * (grad - delta)).astype(BF16)
+        key_grad = nn(r.score_grad[...], self.both_halves(queries, scale, True))
+        keys_t = keys.T * jnp.asarray(scale, BF16)
+        query_parts = []
+        for half in range(2):
+            at = HEAD_DIM * half
+            query_parts.append(
+                nn(keys_t[at : at + HEAD_DIM], r.score_grad[:, space * half : space * half + space])
+            )
+        query_grad = jnp.concatenate(query_parts, 0).T[:rows]
+        r.dqkv[pair][self.rows(s), :256] = jnp.concatenate([query_grad, key_grad], 1).astype(BF16)
+        for other in ((0,), (1, 2), ())[pair]:
+            grads = r.dm[self.rows(s), 128 * other : 128 * other + 128]
+            value_grad = nn(r.pt[3 * s + other], self.both_halves(grads, None, True))
+            r.dqkv[other][self.rows(s), 256:] = value_grad.astype(BF16)
+
+    def project_weight_grad(self, pair):
+        r = self.r
+        target, right = (r.gq0, r.gq1, r.gq2)[pair], r.dqkv[pair][...]
+        if pair == 1:
+            right = jnp.concatenate([right, r.dqkv[2][:, 256:]], 1)
+        if pair == 2:
+            right = right[:, :256]
+        for m in range(2):
+            at = slice(self.half * m, self.half * m + self.half)
+            self.put_blocks(target, 8 * m, tn(r.x_all[:, at], right), self.half // 8)
+
+    def project_bias_grad(self, pair):
+        r = self.r
+        right = r.dqkv[pair]
+        lanes = self.own_lanes(pair)
+        r.gvec[0:1, lanes] = column_sum(right[:, :128].astype(F32))
+        r.gvec[1:2, lanes] = column_sum(right[:, 256:].astype(F32))
+
+    def token_back(self, n, side):
+        r = self.r
+        total = 0.0
+        for pair in range(3):
+            total = total + nt(self.two(r.dqkv[pair], n, side), r.wq[pair][...])
+        return self.by_two(total)
+
+
+def ordered(size):
+    column = iota((1, 8 * size), 1)
+    within = lax.rem(column, 4 * size)
+    source = 2 * size * lax.div(within, size) + size * lax.div(column, 4 * size) + lax.rem(within, size)
+    return iota((8 * size, 8 * size), 0) == source
+
+
+def place_small(r, p):
+    r.small_in[...] = jnp.zeros_like(r.small_in)
+    rows = [(row, 0, vector) for row, vector in enumerate(r.vectors)] + [(0, 128, r.up_bias)]
+    for row, lane, vector in rows:
+        count = vector.shape[0]
+        values = vector[...].reshape(1, count).astype(F32)
+        for core in range(2):
+
+            @pl.when(p == core)
+            def _():
+                at = 2 * row + core
+                r.small_in[at : at + 1, lane : lane + count] = values
+
+
+def pack_square(r, half, piece):
+    at = half * piece
+    for core in range(2):
+        if piece == 3:
+            r.stack[core, :, at : at + half] = r.out_weight[:, half * core : half * core + half].astype(F32)
+            continue
+        for part, weight in enumerate((r.query_weight, r.key_weight, r.value_weight)):
+            lane = half * core + 128 * piece
+            r.stack[core, :, at + 128 * part : at + 128 * part + 128] = weight[:, lane : lane + 128].astype(F32)
+
+
+def pack_up(r, half, size):
+    rows = r.up_weight.shape[0]
+    groups = [r.up_weight[:, 8 * size * group : 8 * size * group + 8 * size] for group in range(CHIPS // 4)]
+    stacked = jnp.concatenate([group.astype(F32) for group in groups], 0).astype(BF16)
+    ordered_units = nn(stacked, ordered(size).astype(BF16))
+    for group in range(CHIPS // 4):
+        to = 4 * half + 4 * size * group
+        for core in range(2):
+            r.stack[core, :, to : to + 4 * size] = ordered_units[
+                rows * group : rows * group + rows, 4 * size * core : 4 * size * core + 4 * size
+            ]
+
+
+def layer_kernel(r):
+    k = Links()
+    p = k.p
+    seqs = r.tokens.shape[0]
+    layer = Layer(r, p)
+    half = layer.half
+    width = layer.width
+    per = r.stack.shape[1]
+    size = r.down_weight.shape[0]
+    pack = r.stack.shape[2]
+    def to_other(src, dst, group, arrival):
+        return pltpu.make_async_remote_copy(
+            src_ref=src,
+            dst_ref=dst,
+            send_sem=r.pair_send.at[group],
+            recv_sem=r.pair_recv.at[arrival],
+            device_id=k.other(),
+            device_id_type=MESH,
+        )
+
+    def local(src, dst, which):
+        return pltpu.make_async_copy(src, dst, r.local_done.at[which])
+
+    def trade_own(ref, group, base):
+        return lambda s: to_other(ref.at[layer.side(s, p)], ref.at[layer.side(s, p)], group, base + s)
+
+    def trade_slot(src, dst, group, base):
+        return lambda s: to_other(src.at[s], dst.at[s], group, base + s)
+
+    def sent(group):
+        to_other(r.part_out, r.part_in, group, 0).wait_send()
+
+    small_swap = to_other(r.small_in, r.small_theirs, 0, 0)
+    share = to_other(r.wo.at[p], r.wo.at[p], 1, 1)
+    sums_swap = to_other(r.sum_small, r.sum_theirs, 2, 2)
+    inputs = lambda s: to_other(r.tokens.at[s, 0], r.x_all.at[layer.side(s, p)], 3, 3)
+    normed = trade_own(r.n_all, 4, 4)
+    down_part = trade_slot(r.part_out, r.part_in, 5, 4 + seqs)
+    down_grad = trade_own(r.dd_all, 6, 4 + 2 * seqs)
+    normed_part = trade_slot(r.part_out, r.part_in, 7, 4 + 3 * seqs)
+    branch = trade_own(r.n_all, 8, 4 + 4 * seqs)
+    token_part = trade_slot(r.part_out, r.part_in, 9, 4 + 5 * seqs)
+
+    def mixed(s, pair):
+        part = r.mixed.at[layer.rows(s), layer.own_lanes(pair)]
+        return to_other(part, part, 10, 4 + 6 * seqs + s)
+
+    def mixed_in(s):
+        part = r.mixed.at[layer.rows(s), block(p, half)]
+        return to_other(part, part, 10, 4 + 6 * seqs + s)
+
+    def pack_swap(lanes):
+        return to_other(r.sum_pack.at[block(1 - p, per), lanes], r.out_pack.at[p, :, lanes], 11, 4 + 7 * seqs)
+
+    pieces = [slice(0, half), slice(half, 2 * half), slice(2 * half, 4 * half)]
+    pieces += [slice(4 * half + lanes.start, 4 * half + lanes.stop) for lanes in UP_LANES]
+
+    def piece_swap(n):
+        lanes = pieces[n]
+        return to_other(
+            r.stack.at[1 - p, :, lanes], r.sum_pack.at[block(p, per), lanes], 12, 5 + 7 * seqs + n
+        )
+
+    def place_piece(n, target):
+        lanes = pieces[n]
+
+        def act():
+            piece_swap(n).wait_recv()
+            r.sum_pack[block(p, per), lanes] = r.stack[p, :, lanes]
+            target[block(k.b, 2 * per)] = r.sum_pack[:, lanes].astype(BF16)
+
+        return act
+
+    def gather(n, ref, near_first=False):
+        return Gather(k, ref, r.gather_send.at[n], r.gather_recv.at[n], near_first)
+
+    def reduce(n, grad, land, near_first=False):
+        return Reduce(k, grad, land, r.reduce_send.at[n], r.reduce_recv.at[n], near_first)
+
+    small = gather(0, r.small_all)
+    heads = [gather(1 + pair, ref) for pair, ref in enumerate((r.wq0, r.wq1, r.wq2o))]
+    ups = [gather(4 + n, r.wup.at[:, lanes], first) for n, (lanes, first) in enumerate(zip(UP_LANES, UP_NEAR_FIRST))]
+    downs = [
+        gather(6 + n, r.wdown.at[:, lanes], first)
+        for n, (lanes, first) in enumerate(zip(DOWN_LANES, DOWN_NEAR_FIRST))
+    ]
+    gathers = [small] + heads + ups + downs
+    down_sums = [
+        reduce(n, r.gd.at[:, lanes], land, first)
+        for n, (lanes, land, first) in enumerate(zip(DOWN_SUM_LANES, r.land_d, DOWN_SUM_NEAR_FIRST))
+    ]
+    up_sums = [
+        reduce(2 + n, r.gu.at[:, lanes], land, first)
+        for n, (lanes, land, first) in enumerate(zip(UP_SUM_LANES, r.land_u, UP_SUM_NEAR_FIRST))
+    ]
+    out_sum = reduce(4, r.goq, r.land_oq)
+    head_sums = [reduce(5, r.gq1, r.land_q1), reduce(6, r.gq2, r.land_q2)]
+    reduces = down_sums + up_sums + [out_sum] + head_sums
+
+    def store(one, lanes):
+        def act():
+            r.sum_pack[:, lanes] = one.result()
+            pack_swap(lanes).start()
+            r.out_pack[p, :, lanes] = r.sum_pack[block(p, per), lanes]
+
+        return act
+
+    def store_down(one, lanes):
+        def act():
+            total = one.result()
+            for group in range(size // per):
+                to = slice(width * group + lanes.start, width * group + lanes.stop)
+                r.out_pack[2, :, to] = total[per * group : per * group + per]
+
+        return act
+
+    def store_last():
+        total = head_sums[1].result()
+        r.sum_pack[:, packs[-1]] = total[: 2 * per]
+        pack_swap(packs[-1]).start()
+        r.sum_small[...] = total[2 * per :]
+        sums_swap.start()
+        r.out_pack[p, :, packs[-1]] = r.sum_pack[block(p, per), packs[-1]]
+
+    packs = [slice(4 * half + lanes.start, 4 * half + lanes.stop) for lanes in UP_SUM_LANES]
+    packs += [slice(0, 2 * half), slice(2 * half, 3 * half + 128), slice(3 * half + 128, 4 * half)]
+    stores = [store_down(one, lanes) for one, lanes in zip(down_sums, DOWN_SUM_LANES)]
+    stores += [store(one, lanes) for one, lanes in zip(up_sums + [out_sum] + head_sums[:1], packs)]
+    stores.append(store_last)
+
+    def place_small_rows():
+        small_swap.wait_recv()
+        r.small_all[block(k.b, 16)] = r.small_in[...] + r.small_theirs[...]
+
+    def finish_out():
+        heads[2].finish()
+        r.wo[p] = r.wq2o[:, half:]
+        share.start()
+
+    starts = [place_small_rows]
+    starts += [place_piece(n, target) for n, target in enumerate((r.wq0, r.wq1, r.wq2o))]
+    starts += [place_piece(3 + n, r.wup.at[:, lanes]) for n, lanes in enumerate(UP_LANES)]
+    spreads = [one.steps() for one in gathers]
+    for steps_of, start in zip(spreads, starts):
+        steps_of[0] = lambda start=start, own=steps_of[0]: (start(), own())
+    sums = [one.steps() + [last] for one, last in zip(reduces, stores)]
+    steps = Steps(seqs, COURSE, spreads + sums)
+
+    k.greet()
+    each(seqs, lambda s: local(r.tokens.at[s, 0], r.x_all.at[layer.side(s, p)], 0).start())
+    local(r.cotangent.at[:, 0], r.out_grad, 1).start()
+    pack_square(r, half, 0)
+    place_small(r, p)
+    k.meet()
+    piece_swap(0).start()
+    small_swap.start()
+    pack_square(r, half, 1)
+    piece_swap(1).start()
+    pack_square(r, half, 2)
+    pack_square(r, half, 3)
+    piece_swap(2).start()
+    pack_up(r, half, size)
+    for n in range(3, len(pieces)):
+        piece_swap(n).start()
+    each(seqs, lambda s: inputs(s).start())
+    r.wdown[block(k.b, size)] = r.down_weight[...]
+    r.gvec[...] = jnp.zeros_like(r.gvec)
+    r.gacc[...] = jnp.zeros_like(r.gacc)
+    r.upg[...] = jnp.zeros_like(r.upg)
+
+    def wait_once(*copies):
+        fresh = [copy for copy in copies if copy not in waited]
+        waited.extend(fresh)
+        return lambda s: [copy(s).wait_recv() for copy in fresh]
+
+    waited = []
+
+    def unpack():
+        def act():
+            each(seqs, layer.mask)
+            small.finish()
+            unpack_small(r, p)
+            to_other(r.part_out, r.part_in, 3, 3).wait_recv()
+            local(r.part_out, r.part_in, 0).wait()
+
+        steps.once(act)
+
+    def attention(pair):
+        def act(s):
+            layer.project(s, pair)
+            layer.attend(s, pair)
+            mixed(s, pair).start()
+
+        steps.loop(act, heads[pair].finish if pair < 2 else finish_out)
+
+    def wait_share():
+        steps.once(lambda: share.wait_recv())
+
+    def first_half():
+        def act(s):
+            mixed_in(s).wait_recv()
+            layer.out_project(s)
+            normed(s).start()
+
+        steps.loop(act)
+
+    def feed(n):
+        wait = wait_once(normed)
+
+        def act(s):
+            wait(s)
+            layer.feed_up(s, UP_LANES[n])
+
+        steps.loop(act, ups[n].finish)
+
+    def feed_other(n):
+        lanes = DOWN_LANES[n]
+
+        def act(two):
+            at = pl.ds(2 * two, 2)
+            r.part_out[at, :, lanes] = layer.feed_down(two, 1 - p, lanes).astype(BF16)
+            if n == len(DOWN_LANES) - 1:
+                for s in range(2):
+                    down_part(2 * two + s).start()
+
+        steps.loop(act, downs[n].finish, seqs // 2)
+
+    def feed_own(n):
+        lanes = DOWN_LANES[n]
+
+        def act(two):
+            r.part_own[pl.ds(2 * two, 2), :, lanes] = layer.feed_down(two, p, lanes)
+
+        steps.loop(act, count=seqs // 2)
+
+    def second_norm():
+        def act(s):
+            down_part(s).wait_recv()
+            layer.finish_norm(s)
+            down_grad(s).start()
+            local(r.final.at[s], r.layer_output.at[s, 0], 2).start()
+
+        steps.loop(act, local(r.cotangent.at[:, 0], r.out_grad, 1).wait)
+
+    def wait_grads():
+        wait = wait_once(down_grad)
+        steps.once(lambda: each(seqs, lambda s: wait(s) and None))
+
+    def down_grads(m):
+        steps.once(lambda: layer.down_weight_grad(m))
+
+    def hidden_back():
+        wait = wait_once(down_grad)
+
+        def act(s):
+            wait(s)
+            layer.hidden_back(s)
+
+        steps.loop(act)
+
+    def up_grads(n):
+        steps.once(lambda: layer.up_weight_grad(n // 2, n % 2))
+
+    def back_other():
+        def first():
+            for group in (4, 5, 6):
+                sent(group)
+
+        def act(two):
+            r.part_out[pl.ds(2 * two, 2)] = layer.normed_back(two, 1 - p).astype(BF16)
+            for s in range(2):
+                normed_part(2 * two + s).start()
+
+        steps.loop(act, first, seqs // 2)
+
+    def back_own():
+        def act(two):
+            r.part_own[pl.ds(2 * two, 2)] = layer.normed_back(two, p)
+
+        steps.loop(act, count=seqs // 2)
+
+    def first_norm():
+        def act(s):
+            normed_part(s).wait_recv()
+            layer.first_norm_back(s)
+            branch(s).start()
+
+        steps.loop(act)
+
+    def mixed_grad():
+        def act(s):
+            branch(s).wait_recv()
+            layer.mixed_back(s)
+
+        steps.loop(act)
+
+    def out_grad():
+        steps.once(layer.out_weight_grad)
+        for one in downs:
+            one.drain()
+
+    def attention_back(pair):
+        steps.loop(lambda s: layer.attend_back(s, pair))
+
+    def head_grads(pair):
+        steps.once(lambda: layer.project_weight_grad(pair))
+
+    def pack_vectors():
+        def act():
+            for pair in range(3):
+                layer.project_bias_grad(pair)
+            pack_small(r, p)
+
+        steps.once(act)
+
+    def token_other():
+        def act(two):
+            r.part_out[pl.ds(2 * two, 2)] = layer.token_back(two, 1 - p).astype(BF16)
+            for s in range(2):
+                token_part(2 * two + s).start()
+
+        steps.loop(act, lambda: sent(7), seqs // 2)
+
+    def token_own():
+        def act(two):
+            r.part_own[pl.ds(2 * two, 2)] = layer.token_back(two, p)
+
+        steps.loop(act, count=seqs // 2)
+
+    def token_end():
+        def first():
+            for one in [small] + heads + ups:
+                one.drain()
+            for copy in (small_swap, share):
+                copy.wait_send()
+            to_other(r.stack.at[1 - p], r.stack.at[p], 12, 0).wait_send()
+            for group in (3, 8, 10):
+                sent(group)
+
+        def act(s):
+            token_part(s).wait_recv()
+            total = r.part_own[s] + r.part_in[s].astype(F32) + r.resid_grad[s]
+            r.token_grad[s] = total.astype(BF16)
+            local(r.token_grad.at[s], r.tokens_gradient.at[s, 0], 3).start()
+
+        steps.loop(act, first)
+
+    def collect():
+        def act():
+            sums_swap.wait_recv()
+            r.out_pack[2, 0:16, pack : pack + 256] = r.sum_small[...] + r.sum_theirs[...]
+            whole = pack_swap(slice(0, pack))
+            whole.wait()
+            for one in reduces:
+                one.drain()
+            sums_swap.wait_send()
+            sent(9)
+            for outgoing in (2, 3):
+                local(r.part_out, r.part_in, outgoing).wait()
+
+        steps.once(act)
+
+    units = dict(
+        unpack=unpack,
+        att=attention,
+        wo=wait_share,
+        out=first_half,
+        up=feed,
+        do=feed_other,
+        dw=feed_own,
+        ln2=second_norm,
+        ddw=wait_grads,
+        gd=down_grads,
+        hb=hidden_back,
+        gu=up_grads,
+        no=back_other,
+        nw=back_own,
+        ln1=first_norm,
+        mb=mixed_grad,
+        go=out_grad,
+        ab=attention_back,
+        gq=head_grads,
+        ps=pack_vectors,
+        to=token_other,
+        tw=token_own,
+        te=token_end,
+        end=collect,
+    )
+    for name, *which in UNITS:
+        units[name](*which)
+    assert not steps.waiting
+
+
+def finish_kernel(r):
+    p = lax.axis_index(PAIR)
+    half = r.query_out.shape[1] // 2
+    size = r.down_out.shape[0]
+    for core in range(2):
+        for pair in range(3):
+            for part, target in enumerate((r.query_out, r.key_out, r.value_out)):
+                place = (0, 1, 2, 6, 7, 8, 10, 11, 9)[3 * pair + part]
+                at, lane = 128 * place, half * core + 128 * pair
+                target[:, lane : lane + 128] = r.pack[core, :, at : at + 128]
+        r.out_out[:, half * core : half * core + half] = r.pack[core, :, half : 2 * half]
+    rows, width = r.query_out.shape
+    groups = []
+    for group in range(CHIPS // 4):
+        at = 4 * half + 4 * size * group
+        groups.append(jnp.concatenate([r.pack[core, :, at : at + 4 * size] for core in range(2)], 1))
+    rest = jnp.concatenate(groups, 0)
+    parts = []
+    for _ in range(3):
+        parts.append(rest.astype(BF16).astype(F32))
+        rest = rest - parts[-1]
+    laid = nt(jnp.concatenate(parts, 0).astype(BF16), ordered(size).astype(BF16))
+    count = laid.shape[0] // 3
+    laid = laid[:count] + laid[count : 2 * count] + laid[2 * count :]
+    for group in range(CHIPS // 4):
+        to = 8 * size * group
+        r.up_out[:, to : to + 8 * size] = laid[rows * group : rows * group + rows]
+    for group in range(size // rows):
+        r.down_out[rows * group : rows * group + rows] = r.pack[2, :, width * group : width * group + width]
+    small = r.pack[2, 0:16, 4 * half + r.up_out.shape[1] // 2 :]
+    for vector, target in enumerate(r.vectors):
+        row = jnp.where(p == 0, small[2 * vector : 2 * vector + 1], small[2 * vector + 1 : 2 * vector + 2])
+        target[...] = row[:, : target.shape[1]]
+    row = jnp.where(p == 0, small[0:1], small[1:2])
+    r.up_vector[...] = row[:, 128 : 128 + size]
+
+
+def call(kernel, ins, outs, scratch, semaphores, elsewhere=(), **params):
+    names = list(ins) + list(outs) + list(scratch) + list(semaphores)
+
+    def body(*refs):
+        kernel(Refs(zip(names, refs)))
+
+    def spec(name):
+        return pl.BlockSpec(memory_space=pl.ANY if name in elsewhere else pltpu.VMEM)
+
+    results = pl.pallas_call(
+        body,
+        out_shape=[jax.ShapeDtypeStruct(*held_as) for held_as in outs.values()],
+        in_specs=[spec(name) for name in ins],
+        out_specs=[spec(name) for name in outs],
+        scratch_shapes=[pltpu.VMEM(*held_as) for held_as in scratch.values()] + list(semaphores.values()),
+        compiler_params=pltpu.CompilerParams(**params),
+        name=kernel.__name__,
+    )(*ins.values())
+    return Refs(zip(outs, results))
+
+
+def fast(
+    tokens,
+    segment_ids,
+    query_weight,
+    query_bias,
+    key_weight,
+    value_weight,
+    value_bias,
+    out_weight,
+    out_bias,
+    first_gain,
+    first_shift,
+    up_weight,
+    up_bias,
+    down_weight,
+    down_bias,
+    second_gain,
+    second_shift,
+    cotangent,
+):
+    seqs, _, slots, width = tokens.shape
+    units = up_weight.shape[1] // 2
+    per = up_weight.shape[0]
+    half = width // 2
+    size = units // CHIPS
+    rows = 2 * slots
+    space = -(-rows // 128) * 128
+    ins = dict(
+        tokens=tokens,
+        cotangent=cotangent,
+        segment_ids=segment_ids,
+        query_weight=query_weight,
+        key_weight=key_weight,
+        value_weight=value_weight,
+        out_weight=out_weight,
+        up_weight=up_weight,
+        down_weight=down_weight,
+        query_bias=query_bias,
+        value_bias=value_bias,
+        out_bias=out_bias,
+        first_gain=first_gain,
+        first_shift=first_shift,
+        down_bias=down_bias,
+        second_gain=second_gain,
+        second_shift=second_shift,
+        up_bias=up_bias,
+    )
+    pack = 4 * half + units
+    outs = dict(
+        layer_output=(tokens.shape, BF16),
+        tokens_gradient=(tokens.shape, BF16),
+        out_pack=((3, per, pack + 256), F32),
+    )
+    all_rows = seqs * rows
+    held = dict(
+        stack=((2, per, pack), F32),
+        sum_pack=((2 * per, pack), F32),
+        small_in=((16, 256), F32),
+        small_theirs=((16, 256), F32),
+        sum_theirs=((16, 256), F32),
+        sum_small=((16, 256), F32),
+        small_all=((CHIPS * 16, 256), F32),
+        vec=((8, width), F32),
+        upb=((1, units), F32),
+        gvec=((8, width), F32),
+        gacc=((64, width), F32),
+        upg=((1, units), F32),
+        fill=((seqs, rows, space), BF16),
+        probs_grad=((2 * rows, space), F32),
+        product=((rows, width), F32),
+        score_grad=((rows, 2 * space), BF16),
+        x_all=((all_rows, width), BF16),
+        wq0=((width, half), BF16),
+        wq1=((width, half), BF16),
+        wq2o=((width, width), BF16),
+        wo=((2, width, half), BF16),
+        wup=((width, units), BF16),
+        wdown=((units, width), BF16),
+        qkv=((3, all_rows, half), BF16),
+        pt=((3 * seqs, rows, 2 * space), BF16),
+        mixed=((all_rows, width), BF16),
+        xhat=((seqs, slots, width), F32),
+        rstd=((seqs, slots, 128), F32),
+        n_all=((all_rows, width), BF16),
+        hidden=((all_rows, units), BF16),
+        slope=((all_rows, units), BF16),
+        part_own=((seqs, slots, width), F32),
+        part_out=((seqs, slots, width), BF16),
+        part_in=((seqs, slots, width), BF16),
+        out_grad=((seqs, slots, width), BF16),
+        final=((seqs, slots, width), BF16),
+        token_grad=((seqs, slots, width), BF16),
+        resid_grad=((seqs, slots, width), F32),
+        dd_all=((all_rows, width), BF16),
+        gd=((units, width), BF16),
+        land_d0=((Reduce.SLOTS * size, DOWN_SUM_LANES[0].stop), BF16),
+        land_d1=((Reduce.SLOTS * size, width - DOWN_SUM_LANES[0].stop), BF16),
+        land_u0=((Reduce.SLOTS * 2 * per, UP_SUM_LANES[0].stop), BF16),
+        land_u1=((Reduce.SLOTS * 2 * per, units - UP_SUM_LANES[0].stop), BF16),
+        land_oq=((Reduce.SLOTS * 2 * per, width), BF16),
+        land_q1=((Reduce.SLOTS * 2 * per, half + 128), BF16),
+        land_q2=((Reduce.SLOTS * (2 * per + 16), half - 128), BF16),
+    )
+    dma = pltpu.SemaphoreType.DMA
+    semaphores = dict(
+        pair_send=dma((13,)),
+        pair_recv=dma((9 + 7 * seqs + len(UP_LANES),)),
+        gather_send=dma((8,)),
+        gather_recv=dma((8, Gather.ARRIVALS)),
+        local_done=dma((4,)),
+        reduce_send=dma((7,)),
+        reduce_recv=dma((7, Reduce.ARRIVALS)),
+    )
+
+    def layer(r):
+        r.gu = r.hidden.at[0:width]
+        last = width + 16 * CHIPS
+        r.goq = r.slope.at[0:width, 0 : 2 * half]
+        split = 3 * half + 128
+        r.gq0 = r.slope.at[0:width, 0:half]
+        r.gq1 = r.slope.at[0:width, 2 * half : split]
+        r.gq2 = r.slope.at[0:last, split : 4 * half]
+        r.go = r.slope.at[0:width, half : 2 * half]
+        r.wq = [r.wq0, r.wq1, r.wq2o.at[:, 0:half]]
+        r.dqkv = [r.wdown.at[0:all_rows, 0:half], r.wdown.at[0:all_rows, half:width], r.dd_all.at[:, 0:half]]
+        r.dm = r.dd_all.at[:, half:width]
+        r.land_d = [r.land_d0, r.land_d1]
+        r.land_u = [r.land_u0, r.land_u1]
+        r.vectors = [
+            r.query_bias,
+            r.value_bias,
+            r.out_bias,
+            r.first_gain,
+            r.first_shift,
+            r.down_bias,
+            r.second_gain,
+            r.second_shift,
+        ]
+        layer_kernel(r)
+
+    elsewhere = dict(tokens=1, cotangent=1, layer_output=1, tokens_gradient=1)
+    done = call(
+        layer, ins, outs, held, semaphores, elsewhere, vmem_limit_bytes=VMEM_BYTES, collective_id=0, has_side_effects=True
+    )
+
+    square = ((per, width), F32)
+    line = ((1, per), F32)
+    finals = dict(
+        query_out=square,
+        query_vector=line,
+        key_out=square,
+        value_out=square,
+        value_vector=line,
+        out_out=square,
+        out_vector=line,
+        gain_vector=line,
+        shift_vector=line,
+        up_out=(up_weight.shape, F32),
+        up_vector=((1, size), F32),
+        down_out=(down_weight.shape, F32),
+        down_vector=line,
+        last_gain_vector=line,
+        last_shift_vector=line,
+    )
+
+    def finish(r):
+        r.vectors = [
+            r.query_vector,
+            r.value_vector,
+            r.out_vector,
+            r.gain_vector,
+            r.shift_vector,
+            r.down_vector,
+            r.last_gain_vector,
+            r.last_shift_vector,
+        ]
+        finish_kernel(r)
+
+    final = call(finish, dict(pack=done.out_pack), finals, {}, {}, vmem_limit_bytes=16 * 1024 * 1024)
+    flat = [value[0] if value.shape[0] == 1 else value for value in final.values()]
+    return (done.layer_output, done.tokens_gradient, *flat)
+
+
 def solution(mesh):
     in_specs = (
-        P("batch", "pair", None, None),
-        P("batch", None, None),
-        P(("batch", "pair"), None),
-        P(("batch", "pair")),
-        P(("batch", "pair"), None),
-        P(("batch", "pair"), None),
-        P(("batch", "pair")),
-        P(("batch", "pair"), None),
-        P(("batch", "pair")),
-        P(("batch", "pair")),
-        P(("batch", "pair")),
-        P(("batch", "pair"), None),
-        P(("batch", "pair")),
-        P(("batch", "pair"), None),
-        P(("batch", "pair")),
-        P(("batch", "pair")),
-        P(("batch", "pair")),
-        P("batch", "pair", None, None),
+        P(BATCH, PAIR, None, None),
+        P(BATCH, None, None),
+        P(AXES, None),
+        P(AXES),
+        P(AXES, None),
+        P(AXES, None),
+        P(AXES),
+        P(AXES, None),
+        P(AXES),
+        P(AXES),
+        P(AXES),
+        P(AXES, None),
+        P(AXES),
+        P(AXES, None),
+        P(AXES),
+        P(AXES),
+        P(AXES),
+        P(BATCH, PAIR, None, None),
     )
     out_specs = (
-        P("batch", "pair", None, None),
-        P("batch", "pair", None, None),
-        P(("batch", "pair"), None),
-        P(("batch", "pair")),
-        P(("batch", "pair"), None),
-        P(("batch", "pair"), None),
-        P(("batch", "pair")),
-        P(("batch", "pair"), None),
-        P(("batch", "pair")),
-        P(("batch", "pair")),
-        P(("batch", "pair")),
-        P(("batch", "pair"), None),
-        P(("batch", "pair")),
-        P(("batch", "pair"), None),
-        P(("batch", "pair")),
-        P(("batch", "pair")),
-        P(("batch", "pair")),
-    )
-    return jax.shard_map(local, mesh=mesh, in_specs=in_specs, out_specs=out_specs, check_vma=False)
+        P(BATCH, PAIR, None, None),
+        P(BATCH, PAIR, None, None),
+        P(AXES, None),
+        P(AXES),
+        P(AXES, None),
+        P(AXES, None),
+        P(AXES),
+        P(AXES, None),
+        P(AXES),
+        P(AXES),
+        P(AXES),
+        P(AXES, None),
+        P(AXES),
+        P(AXES, None),
+        P(AXES),
+        P(AXES),
+        P(AXES),
+    )
+    small_slice = dict(mesh.shape) == {BATCH: CHIPS, PAIR: 2}
+    part = fast if small_slice else local
+    return jax.shard_map(part, mesh=mesh, in_specs=in_specs, out_specs=out_specs, check_vma=False)

time: 1110 us -> 154 us (0.14)
  waiting for transfers between devices: 798 us -> 0 us
  Pallas kernels: 0 us -> 150 us
  matrix products: 119 us -> 0 us
  blocking collectives: 83.4 us -> 0 us
  local copies, waits for them, and re-layouts: 59.1 us -> 3.68 us
  other arithmetic: 26.4 us -> 0 us
  between operations: 15.2 us -> 0.69 us
    reduce_scatter x3 -> x0, waiting for transfers between devices: 283 us -> none  [the longest x1 142 us: local(): lax.psum_scatter(feedforward_terms[0], ('batch', 'pair'), scatter_dimensi...]
    all_gather x6 -> x0, waiting for transfers between devices: 260 us -> none  [the longest x1 61.8 us: local(): lax.all_gather(feedforward_shards[0], ('batch', 'pair'), axis=0, tiled=True)]
    unnamed x15 -> x0, waiting for transfers between devices: 256 us -> none
    pallas_call x0 -> x2, Pallas kernels: none -> 150 us  [call(): pl.pallas_call(body, out_shape=[jax.ShapeDtypeStruct(*held_as) for held_a...]
    dot_general x24 -> x0, matrix products: 119 us -> none  [the longest x6 29.3 us: outer_sum(): lax.dot_general(flat_left, flat_right, (((0,), (0,)), ((), ())), preferre...]
    unnamed x2 -> x0, blocking collectives: 83.4 us -> none
    unnamed x120 -> x8, local copies, waits for them, and re-layouts: 39.7 us -> 3.68 us
    reduce_sum x9 -> x0, other arithmetic: 14.1 us -> none  [the longest x3 5.97 us: row_total(): return jnp.sum(values.astype(jnp.float32), (0, 1))]
  transfers between devices with their start and end apart: 16 -> 0, of which waited for: 11 -> 0; matrix products, arithmetic and copies ran while one was open for 14% -> 0% of each run, Pallas kernels for 0% -> 0%
where the time goes in v1:
time: 154 us
  Pallas kernels  150 us (97%)
  local copies, waits for them, and re-layouts  3.68 us (2%)
    pallas_call x2, Pallas kernels, call(): pl.pallas_call(body, out_shape=[jax.ShapeDtypeStruct(*held_as) for held_a...  150 us
    unnamed x8, local copies, waits for them, and re-layouts  3.68 us

profile of v1, /device:TPU:0, one launch (start us, length us, event | category | flops | bytes accessed | tf_op | source)
XLA Modules:
  0.0 154.2 jit_solution(4140260645894395424)
XLA Ops:
  0.7 148.5 %layer.1 = (bf16[4,1,160,768]{3,2,1,0:T(8,128)(2,1)}, bf16[4,1,160,768]{3,2,1,0:T(8,128)(2,1)}, f32[3,24,3328]{2,1,0:T(8,128)}) custom-call(bf16[4,1,160,768]{3,2,1,0:T(8,128)(2,1)} %refs_0_.1, bf16[4,1,160,768]{3,2,1,0:T(8,128)(2,1)} %refs_1_.1, s32[4,2,160]{2,1,0:T(2,128)} %refs_2_.1, bf16[24,768]{1,0:T(8,128)(2,1)} %refs_3_.1, bf16[24,768]{1,0:T(8,128)(2,1)} %refs_4_.1, ...), custom_call_target="tpu_custom_call" | custom-call | tf_op jit(solution)/shard_map/layer/pallas_call | solution.py:1524
  149.2 0.0 copy-start
  149.2 1.2 copy-done
  150.3 0.0 copy-start.2
  150.3 1.4 finish.1
  151.7 0.0 copy-done.2
  151.7 0.0 copy-start.1
  151.7 0.9 copy.37
  152.7 0.6 copy-done.1
  153.3 0.9 copy.38
Async XLA Ops:
  149.2 1.2 copy-start
  150.3 1.4 copy-start.2
  151.7 1.6 %copy-start.1 = (bf16[4,1,160,768]{3,2,1,0:T(8,128)(2,1)S(1)}, bf16[4,1,160,768]{3,2,1,0:T(8,128)(2,1)}, u32[]{:S(2)}) copy-start(bf16[4,1,160,768]{3,2,1,0:T(8,128)(2,1)} %get-tuple-element.71) | copy-start | bytes 2949124

commit v2 on v1

--- a/solution.py
+++ b/solution.py
@@ -687,6 +687,8 @@
 DOWN_SUM_LANES = (slice(0, 512), slice(512, 768),)
 DOWN_SUM_NEAR_FIRST = (False, True)
 UNITS = (
+    ("sa",),
+    ("sb",),
     ("unpack",),
     ("att", 0),
     ("att", 1),
@@ -696,10 +698,11 @@
     ("up", 0),
     ("up", 1),
     ("do", 0),
+    ("do", 1),
     ("dw", 0),
-    ("do", 1),
     ("dw", 1),
     ("ln2",),
+    ("ge",),
     ("ddw",),
     ("gd", 0),
     ("gd", 1),
@@ -728,52 +731,50 @@
     ("end",),
 )
 COURSE = {
-    0: (0, 1, 2, 3, 0, 0, 2, 4, 0, 0, 3, 1, 1, 6, 2, 1, 0, 0, 1, 3, 0, 1, 1, 5, 1, 2, 2, 3, 3,),
-    1: (2, 4, 2,),
-    2: (4,),
-    3: (2, 3, 3,),
-    4: (4, 4, 5,),
-    6: (6, 3,),
-    7: (6,),
-    8: (4, 4, 7,),
+    0: (6,),
+    1: (0, 1, 2, 3, 1, 6, 6, 2,),
+    2: (3, 4, 0, 0, 7, 1, 5, 1, 1, 2, 0, 0, 1, 1, 2, 0, 0, 2, 3, 0, 1, 4, 2, 2, 3, 3, 6,),
+    5: (2, 5,),
+    6: (3, 3,),
+    8: (4,),
+    9: (3,),
     10: (6,),
-    12: (6, 5,),
-    15: (4,),
-    16: (5, 5,),
-    17: (5, 5, 6,),
-    18: (5, 6, 7, 7,),
-    23: (6,),
-    24: (7, 7,),
-    25: (7, 7, 7,),
-    40: (9,),
-    41: (9,),
-    42: (9,),
+    11: (4, 4,),
+    13: (6,),
+    14: (4, 4, 7, 6,),
+    17: (4, 5,),
+    19: (5,),
+    20: (5, 5, 5, 5, 7,),
+    24: (6, 7, 7, 7, 7, 7,),
     43: (9,),
-    44: (8,),
-    45: (8, 8, 8, 9,),
-    48: (9,),
-    49: (9, 9, 9, 8,),
-    50: (8, 8,),
-    52: (8, 10, 10, 10,),
-    55: (8, 9,),
-    59: (10, 11,),
-    60: (11, 8,),
-    63: (8, 11, 11,),
-    65: (10,),
-    67: (10, 11, 10, 10, 10, 10, 11,),
-    68: (11,),
-    69: (12, 11,),
-    70: (12,),
-    72: (12, 12, 12,),
-    74: (11,),
-    75: (12, 12, 12, 13, 11,),
-    77: (11, 13, 13, 13,),
-    79: (12, 12, 12, 13,),
-    80: (14, 13,),
-    81: (13, 13, 14, 14, 8, 14,),
-    83: (9, 13, 13, 13, 14, 14,),
-    85: (14, 14, 14, 14, 14, 12, 10,),
-    86: (9, 11, 10, 13, 14,),
+    44: (9, 8,),
+    46: (8, 9, 9, 8,),
+    49: (8,),
+    52: (9, 9,),
+    53: (9, 9, 9, 8, 8, 8,),
+    55: (8, 10, 10,),
+    58: (10, 10, 8,),
+    60: (9,),
+    62: (8, 11, 11,),
+    63: (8,),
+    65: (11,),
+    68: (10, 10, 10, 9,),
+    69: (11, 11, 11,),
+    72: (12, 10, 10, 10, 12, 11, 11,),
+    75: (12, 12, 12, 12,),
+    76: (11,),
+    77: (13, 11,),
+    78: (12,),
+    79: (9, 11, 12, 13, 13, 13,),
+    82: (13, 12, 12,),
+    83: (14, 12, 14, 13,),
+    84: (13, 13, 14, 14,),
+    85: (11,),
+    87: (14, 13, 14, 14, 8, 14, 13, 12, 10,),
+    88: (13,),
+    89: (14,),
+    90: (14, 10,),
+    91: (14, 13, 14,),
 }
 
 
@@ -921,10 +922,20 @@
             rows = pl.ds(pl.multiple_of(at + self.p * step * space, 16), size) if step else slice(at, at + size)
             ref[rows] = low[n * size : n * size + size]
 
+    def first_down_weight_grad(self):
+        r = self.r
+        most = slice(0, r.hidden.shape[0] - 2 * self.slots)
+        r.first_sum[...] = tn(r.hidden[most, : self.half], r.dd_all[most])
+
     def down_weight_grad(self, m):
         r = self.r
         at = slice(self.half * m, self.half * m + self.half)
-        self.put_blocks(r.gd, 4 * m, tn(r.hidden[:, at], r.dd_all[...]), self.half // 4)
+        if m == 0:
+            last = slice(r.hidden.shape[0] - 2 * self.slots, r.hidden.shape[0])
+            total = r.first_sum[...] + tn(r.hidden[last, at], r.dd_all[last])
+        else:
+            total = tn(r.hidden[:, at], r.dd_all[...])
+        self.put_blocks(r.gd, 4 * m, total, self.half // 4)
 
     def hidden_back(self, s):
         r = self.r
@@ -1233,24 +1244,12 @@
     k.greet()
     each(seqs, lambda s: local(r.tokens.at[s, 0], r.x_all.at[layer.side(s, p)], 0).start())
     local(r.cotangent.at[:, 0], r.out_grad, 1).start()
+    r.wdown[block(k.b, size)] = r.down_weight[...]
     pack_square(r, half, 0)
     place_small(r, p)
     k.meet()
     piece_swap(0).start()
     small_swap.start()
-    pack_square(r, half, 1)
-    piece_swap(1).start()
-    pack_square(r, half, 2)
-    pack_square(r, half, 3)
-    piece_swap(2).start()
-    pack_up(r, half, size)
-    for n in range(3, len(pieces)):
-        piece_swap(n).start()
-    each(seqs, lambda s: inputs(s).start())
-    r.wdown[block(k.b, size)] = r.down_weight[...]
-    r.gvec[...] = jnp.zeros_like(r.gvec)
-    r.gacc[...] = jnp.zeros_like(r.gacc)
-    r.upg[...] = jnp.zeros_like(r.upg)
 
     def wait_once(*copies):
         fresh = [copy for copy in copies if copy not in waited]
@@ -1258,6 +1257,27 @@
         return lambda s: [copy(s).wait_recv() for copy in fresh]
 
     waited = []
+
+    def pack_heads():
+        def act():
+            pack_square(r, half, 1)
+            piece_swap(1).start()
+            pack_square(r, half, 2)
+            pack_square(r, half, 3)
+            piece_swap(2).start()
+
+        steps.once(act)
+
+    def pack_rest():
+        def act():
+            pack_up(r, half, size)
+            for n in range(3, len(pieces)):
+                piece_swap(n).start()
+            each(seqs, lambda s: inputs(s).start())
+            for sums in (r.gvec, r.gacc, r.upg):
+                sums[...] = jnp.zeros_like(sums)
+
+        steps.once(act)
 
     def unpack():
         def act():
@@ -1326,9 +1346,16 @@
 
         steps.loop(act, local(r.cotangent.at[:, 0], r.out_grad, 1).wait)
 
+    def first_down_grads():
+        def act():
+            each(seqs - 1, lambda s: down_grad(s).wait_recv())
+            layer.first_down_weight_grad()
+
+        waited.append(down_grad)
+        steps.once(act)
+
     def wait_grads():
-        wait = wait_once(down_grad)
-        steps.once(lambda: each(seqs, lambda s: wait(s) and None))
+        steps.once(lambda: down_grad(seqs - 1).wait_recv())
 
     def down_grads(m):
         steps.once(lambda: layer.down_weight_grad(m))
@@ -1445,6 +1472,9 @@
         steps.once(act)
 
     units = dict(
+        sa=pack_heads,
+        sb=pack_rest,
+        ge=first_down_grads,
         unpack=unpack,
         att=attention,
         wo=wait_share,
@@ -1628,6 +1658,7 @@
         resid_grad=((seqs, slots, width), F32),
         dd_all=((all_rows, width), BF16),
         gd=((units, width), BF16),
+        first_sum=((half, width), F32),
         land_d0=((Reduce.SLOTS * size, DOWN_SUM_LANES[0].stop), BF16),
         land_d1=((Reduce.SLOTS * size, width - DOWN_SUM_LANES[0].stop), BF16),
         land_u0=((Reduce.SLOTS * 2 * per, UP_SUM_LANES[0].stop), BF16),

time: 154 us -> 155 us (level)
  no operation moved by 1% of the time
where the time goes in v2:
time: 155 us
  Pallas kernels  151 us (97%)
  local copies, waits for them, and re-layouts  3.68 us (2%)
    pallas_call x2, Pallas kernels, call(): pl.pallas_call(body, out_shape=[jax.ShapeDtypeStruct(*held_as) for held_a...  151 us
    unnamed x8, local copies, waits for them, and re-layouts  3.68 us

profile of v2, /device:TPU:0, one launch (start us, length us, event | category | flops | bytes accessed | tf_op | source)
XLA Modules:
  0.0 155.1 jit_solution(7938544887511412840)
XLA Ops:
  0.7 149.4 %layer.1 = (bf16[4,1,160,768]{3,2,1,0:T(8,128)(2,1)}, bf16[4,1,160,768]{3,2,1,0:T(8,128)(2,1)}, f32[3,24,3328]{2,1,0:T(8,128)}) custom-call(bf16[4,1,160,768]{3,2,1,0:T(8,128)(2,1)} %refs_0_.1, bf16[4,1,160,768]{3,2,1,0:T(8,128)(2,1)} %refs_1_.1, s32[4,2,160]{2,1,0:T(2,128)} %refs_2_.1, bf16[24,768]{1,0:T(8,128)(2,1)} %refs_3_.1, bf16[24,768]{1,0:T(8,128)(2,1)} %refs_4_.1, ...), custom_call_target="tpu_custom_call" | custom-call | tf_op jit(solution)/shard_map/layer/pallas_call | solution.py:1554
  150.0 0.0 copy-start
  150.0 1.2 copy-done
  151.2 0.0 copy-start.2
  151.2 1.4 finish.1
  152.6 0.0 copy-done.2
  152.6 0.0 copy-start.1
  152.6 0.9 copy.37
  153.6 0.6 copy-done.1
  154.2 0.9 copy.38
Async XLA Ops:
  150.0 1.2 copy-start
  151.2 1.4 copy-start.2
  152.6 1.6 %copy-start.1 = (bf16[4,1,160,768]{3,2,1,0:T(8,128)(2,1)S(1)}, bf16[4,1,160,768]{3,2,1,0:T(8,128)(2,1)}, u32[]{:S(2)}) copy-start(bf16[4,1,160,768]{3,2,1,0:T(8,128)(2,1)} %get-tuple-element.71) | copy-start | bytes 2949124

commit v3 on v2

--- a/solution.py
+++ b/solution.py
@@ -732,49 +732,48 @@
 )
 COURSE = {
     0: (6,),
-    1: (0, 1, 2, 3, 1, 6, 6, 2,),
-    2: (3, 4, 0, 0, 7, 1, 5, 1, 1, 2, 0, 0, 1, 1, 2, 0, 0, 2, 3, 0, 1, 4, 2, 2, 3, 3, 6,),
-    5: (2, 5,),
-    6: (3, 3,),
-    8: (4,),
-    9: (3,),
-    10: (6,),
-    11: (4, 4,),
-    13: (6,),
-    14: (4, 4, 7, 6,),
-    17: (4, 5,),
-    19: (5,),
-    20: (5, 5, 5, 5, 7,),
-    24: (6, 7, 7, 7, 7, 7,),
-    43: (9,),
-    44: (9, 8,),
-    46: (8, 9, 9, 8,),
+    1: (0, 3, 1,),
+    2: (2, 6, 4, 6, 4, 5, 6, 6, 0, 0, 3, 3, 1, 0, 0, 2, 7, 1, 3, 3, 2, 1, 1, 0, 3, 0, 2, 2, 1, 1, 0, 3, 2, 1, 2, 4,),
+    3: (6,),
+    4: (2, 3,),
+    5: (4, 4,),
+    6: (5,),
+    8: (7, 7,),
+    9: (5,),
+    10: (4, 4,),
+    11: (6,),
+    13: (5,),
+    15: (4,),
+    17: (5, 5, 5,),
+    18: (5,),
+    20: (7, 7, 6,),
+    22: (7, 7, 7,),
+    43: (8,),
+    45: (9, 9, 9,),
+    46: (9,),
     49: (8,),
-    52: (9, 9,),
-    53: (9, 9, 9, 8, 8, 8,),
-    55: (8, 10, 10,),
-    58: (10, 10, 8,),
-    60: (9,),
-    62: (8, 11, 11,),
-    63: (8,),
-    65: (11,),
-    68: (10, 10, 10, 9,),
-    69: (11, 11, 11,),
-    72: (12, 10, 10, 10, 12, 11, 11,),
-    75: (12, 12, 12, 12,),
-    76: (11,),
-    77: (13, 11,),
-    78: (12,),
-    79: (9, 11, 12, 13, 13, 13,),
-    82: (13, 12, 12,),
-    83: (14, 12, 14, 13,),
-    84: (13, 13, 14, 14,),
-    85: (11,),
-    87: (14, 13, 14, 14, 8, 14, 13, 12, 10,),
-    88: (13,),
-    89: (14,),
-    90: (14, 10,),
-    91: (14, 13, 14,),
+    52: (10,),
+    54: (10, 10, 10, 9,),
+    55: (9, 9, 9, 9, 9,),
+    56: (11, 11, 11,),
+    63: (11,),
+    64: (10, 10, 10, 10, 10, 10,),
+    66: (11,),
+    67: (8,),
+    69: (11, 11, 11, 8,),
+    72: (12, 11, 11, 8, 8, 8, 8,),
+    74: (12, 11,),
+    76: (12, 12, 12, 8, 8, 8,),
+    78: (13,),
+    80: (12,),
+    81: (12, 11, 12,),
+    83: (13, 13, 13, 13, 14, 14,),
+    84: (12, 12, 12,),
+    85: (13, 13, 13, 14, 14, 14, 10, 13, 13, 14, 14, 13, 14, 8,),
+    88: (12,),
+    89: (9, 14,),
+    90: (14, 14, 10,),
+    91: (13, 9, 14,),
 }
 
 

time: 155 us -> 157 us (1.013)
  no operation moved by 1% of the time
where the time goes in v3:
time: 157 us
  Pallas kernels  152 us (97%)
  local copies, waits for them, and re-layouts  3.68 us (2%)
    pallas_call x2, Pallas kernels, call(): pl.pallas_call(body, out_shape=[jax.ShapeDtypeStruct(*held_as) for held_a...  152 us
    unnamed x8, local copies, waits for them, and re-layouts  3.68 us

profile of v3, /device:TPU:0, one launch (start us, length us, event | category | flops | bytes accessed | tf_op | source)
XLA Modules:
  0.0 156.6 jit_solution(16131372892231541070)
XLA Ops:
  0.7 150.8 %layer.1 = (bf16[4,1,160,768]{3,2,1,0:T(8,128)(2,1)}, bf16[4,1,160,768]{3,2,1,0:T(8,128)(2,1)}, f32[3,24,3328]{2,1,0:T(8,128)}) custom-call(bf16[4,1,160,768]{3,2,1,0:T(8,128)(2,1)} %refs_0_.1, bf16[4,1,160,768]{3,2,1,0:T(8,128)(2,1)} %refs_1_.1, s32[4,2,160]{2,1,0:T(2,128)} %refs_2_.1, bf16[24,768]{1,0:T(8,128)(2,1)} %refs_3_.1, bf16[24,768]{1,0:T(8,128)(2,1)} %refs_4_.1, ...), custom_call_target="tpu_custom_call" | custom-call | tf_op jit(solution)/shard_map/layer/pallas_call | solution.py:1553
  151.5 0.0 copy-start
  151.5 1.2 copy-done
  152.7 0.0 copy-start.2
  152.7 1.4 finish.1
  154.0 0.0 copy-done.2
  154.1 0.0 copy-start.1
  154.1 0.9 copy.37
  155.0 0.6 copy-done.1
  155.6 0.9 copy.38
Async XLA Ops:
  151.5 1.2 copy-start
  152.7 1.4 copy-start.2
  154.1 1.6 copy-start.1

commit v4 on v1

--- a/solution.py
+++ b/solution.py
@@ -921,10 +921,20 @@
             rows = pl.ds(pl.multiple_of(at + self.p * step * space, 16), size) if step else slice(at, at + size)
             ref[rows] = low[n * size : n * size + size]
 
+    def first_down_weight_grad(self):
+        r = self.r
+        most = slice(0, r.hidden.shape[0] - 2 * self.slots)
+        r.first_sum[...] = tn(r.hidden[most, : self.half], r.dd_all[most])
+
     def down_weight_grad(self, m):
         r = self.r
         at = slice(self.half * m, self.half * m + self.half)
-        self.put_blocks(r.gd, 4 * m, tn(r.hidden[:, at], r.dd_all[...]), self.half // 4)
+        if m == 0:
+            last = slice(r.hidden.shape[0] - 2 * self.slots, r.hidden.shape[0])
+            total = r.first_sum[...] + tn(r.hidden[last, at], r.dd_all[last])
+        else:
+            total = tn(r.hidden[:, at], r.dd_all[...])
+        self.put_blocks(r.gd, 4 * m, total, self.half // 4)
 
     def hidden_back(self, s):
         r = self.r
@@ -1327,8 +1337,13 @@
         steps.loop(act, local(r.cotangent.at[:, 0], r.out_grad, 1).wait)
 
     def wait_grads():
-        wait = wait_once(down_grad)
-        steps.once(lambda: each(seqs, lambda s: wait(s) and None))
+        def act():
+            each(seqs - 1, lambda s: down_grad(s).wait_recv())
+            layer.first_down_weight_grad()
+            down_grad(seqs - 1).wait_recv()
+
+        waited.append(down_grad)
+        steps.once(act)
 
     def down_grads(m):
         steps.once(lambda: layer.down_weight_grad(m))
@@ -1628,6 +1643,7 @@
         resid_grad=((seqs, slots, width), F32),
         dd_all=((all_rows, width), BF16),
         gd=((units, width), BF16),
+        first_sum=((half, width), F32),
         land_d0=((Reduce.SLOTS * size, DOWN_SUM_LANES[0].stop), BF16),
         land_d1=((Reduce.SLOTS * size, width - DOWN_SUM_LANES[0].stop), BF16),
         land_u0=((Reduce.SLOTS * 2 * per, UP_SUM_LANES[0].stop), BF16),

time: 154 us -> 154 us (level)
  no operation moved by 1% of the time
where the time goes in v4:
time: 154 us
  Pallas kernels  150 us (97%)
  local copies, waits for them, and re-layouts  3.68 us (2%)
    pallas_call x2, Pallas kernels, call(): pl.pallas_call(body, out_shape=[jax.ShapeDtypeStruct(*held_as) for held_a...  150 us
    unnamed x8, local copies, waits for them, and re-layouts  3.68 us

profile of v4, /device:TPU:0, one launch (start us, length us, event | category | flops | bytes accessed | tf_op | source)
XLA Modules:
  0.0 153.9 jit_solution(16380268295788682748)
XLA Ops:
  0.7 148.1 %layer.1 = (bf16[4,1,160,768]{3,2,1,0:T(8,128)(2,1)}, bf16[4,1,160,768]{3,2,1,0:T(8,128)(2,1)}, f32[3,24,3328]{2,1,0:T(8,128)}) custom-call(bf16[4,1,160,768]{3,2,1,0:T(8,128)(2,1)} %refs_0_.1, bf16[4,1,160,768]{3,2,1,0:T(8,128)(2,1)} %refs_1_.1, s32[4,2,160]{2,1,0:T(2,128)} %refs_2_.1, bf16[24,768]{1,0:T(8,128)(2,1)} %refs_3_.1, bf16[24,768]{1,0:T(8,128)(2,1)} %refs_4_.1, ...), custom_call_target="tpu_custom_call" | custom-call | tf_op jit(solution)/shard_map/layer/pallas_call | solution.py:1539
  148.8 0.0 copy-start
  148.8 1.2 copy-done
  150.0 0.0 copy-start.2
  150.0 1.4 finish.1
  151.4 0.0 copy-done.2
  151.4 0.0 copy-start.1
  151.4 0.9 copy.37
  152.3 0.6 copy-done.1
  152.9 0.9 copy.38
Async XLA Ops:
  148.8 1.2 copy-start
  150.0 1.4 copy-start.2
  151.4 1.6 %copy-start.1 = (bf16[4,1,160,768]{3,2,1,0:T(8,128)(2,1)S(1)}, bf16[4,1,160,768]{3,2,1,0:T(8,128)(2,1)}, u32[]{:S(2)}) copy-start(bf16[4,1,160,768]{3,2,1,0:T(8,128)(2,1)} %get-tuple-element.71) | copy-start | bytes 2949124
